TPU v7x, 512 devices: a whole 4x8x8 slice. The times are simulated.
512 devices in a mesh: ctx: 32 (over z, x_lo, core), ch: 16 (over y, x_hi).
Axes of the slice: x: 4 (x_hi: 2, x_lo: 2; x = x_hi * 2 + x_lo), y: 8, z: 8, core: 2. Of those that a mesh axis runs over, the one named last changes fastest.
Arguments:
- q_stream: bfloat16 [8192, 8192], P('ctx', 'ch'), may hold values from -6 to 6
- k_stream: bfloat16 [8192, 8192], P('ctx', 'ch'), may hold values from -50 to 50
- v_stream: bfloat16 [8192, 8192], P('ctx', 'ch'), may hold values from -6 to 6
- filters: float32 [8192, 8192], P('ctx', 'ch'), may hold values from -3 to 3
- norm_gain: float32 [8192], replicated, may hold values from 0.4 to 1.6
Outputs:
- block_out: bfloat16 [8192, 8192], P(('ctx', 'ch'))
All inputs are finite; a program needn't handle non-finite values.
Results may differ from a plain program's by a relative error of at most 0.017.
Values may be sent and summed in bfloat16 or wider, within the bound.
No kernel may reach another device: no remote copies, remote signals or barrier semaphores. Data moves between devices by JAX's collectives and lax.ppermute only.
A program may use at most 64 MiB of HBM per device.

v0:
```python
import functools
import math

import jax
import jax.numpy as jnp
import numpy as np
from jax import lax
from jax.experimental import pallas as pl
from jax.experimental.pallas import tpu as pltpu
from jax.sharding import PartitionSpec as P

BF16 = jnp.bfloat16
F32 = jnp.float32
VMEM_BYTES = 40 * 2**20


def parts_of(table):
    high = table.astype(np.float32).astype(jnp.bfloat16)
    low = (table - high.astype(np.float64)).astype(np.float32).astype(jnp.bfloat16)
    return high, low


def stacked_table(matrix):
    table = np.block([[matrix.real, matrix.imag], [-matrix.imag, matrix.real]])
    high, low = parts_of(table)
    return np.concatenate([high, low], axis=0)


def inner_tables(tok_rows):
    half = np.arange(tok_rows // 2)
    even_turns = 2 * half[:, None] * half[None, :] % tok_rows
    odd_turns = half[:, None] * (2 * half[None, :] + 1) % tok_rows
    even, odd = (
        np.exp(-2j * np.pi * turns / tok_rows) for turns in (even_turns, odd_turns)
    )
    return stacked_table(even), stacked_table(odd), stacked_table(odd.T)


def outer_tables(blocks, tok_rows, lines, order_in, order_out):
    index = np.arange(blocks)
    freqs = np.arange(blocks + 1)
    angle = np.pi * (freqs[:, None] * index[None, :] % (2 * blocks)) / blocks
    forward = np.concatenate([np.cos(angle), -np.sin(angle)[1:blocks]], axis=0)
    weight = np.full((2 * blocks, 1), 2.0 / (2 * blocks * tok_rows))
    weight[0] *= 0.5
    weight[blocks] *= 0.5
    backward = (weight * forward).T
    apart = np.eye(lines)
    return (
        np.concatenate(parts_of(np.kron(forward[:, order_in], apart)), axis=1),
        *parts_of(np.kron(backward[order_out], apart)),
    )


def twist_tables(blocks, tok_rows):
    period = 2 * blocks * tok_rows
    index = np.arange(blocks + 1)[:, None] * np.arange(tok_rows)[None, :] % period
    angle = 2.0 * np.pi * index / period
    return np.cos(angle).astype(np.float32), np.sin(angle).astype(np.float32)


def mix_kernel(order, k_hbm, v_hbm, filters_hbm, out_ref, k_ref, v_ref, filters_ref, sems):
    groups, rows, tok_rows = out_ref.shape
    width = rows // 2
    half = tok_rows // 2
    halves = (slice(0, half), slice(half, tok_rows))
    pairs = [(k_hbm, k_ref), (v_hbm, v_ref)]
    pairs += [(filters_hbm.at[at], filters_ref.at[at]) for at in halves]
    copies = [
        pltpu.make_async_copy(source, target, sems.at[n])
        for n, (source, target) in enumerate(pairs)
    ]
    for copy in copies:
        copy.start()
    copies[0].wait()
    copies[1].wait()
    mixed = (k_ref[...].astype(F32) * v_ref[...].astype(F32)).T
    mixed = mixed.reshape(groups, width, tok_rows).astype(BF16)
    for n, group in enumerate(order):
        out_ref[n, :width] = mixed[group]
    for at, copy in zip(halves, copies[2:]):
        copy.wait()
        taps = filters_ref[at].T.reshape(groups, width, half).astype(BF16)
        for n, group in enumerate(order):
            out_ref[n, width:, at] = taps[group]


def split_parts(values):
    high = values.astype(BF16)
    return high, (values - high.astype(F32)).astype(BF16)


def inner_dft(high, low, table_ref):
    left = jnp.concatenate([high, low, high], axis=1)
    table = table_ref[...]
    right = jnp.concatenate([table[: high.shape[1]], table], axis=0)
    return jnp.dot(left, right, preferred_element_type=F32)


def conv_kernel(
    in_ref, twist_ref, inner_ref, outer_ref, out_ref,
    outer, even_high, even_low, odd_high, odd_low, even, odd,
):
    blocks, rows, tok_rows = in_ref.shape
    width = rows // 2
    half = tok_rows // 2
    first, second = slice(0, half), slice(half, tok_rows)
    lines = 8
    subs = range(width // lines)
    real_rows = (blocks + 1) * lines
    cos_ref, sin_ref = twist_ref.at[0], twist_ref.at[1]
    even_ref, odd_ref, back_ref = (inner_ref.at[n] for n in range(3))
    back_rows = blocks * lines
    high_ref = outer_ref.at[2 * back_rows : 3 * back_rows]
    low_ref = outer_ref.at[3 * back_rows : 4 * back_rows]

    def of_freq(k, start=0):
        return slice(start + k * lines, start + (k + 1) * lines)

    def outer_dft(stream):
        top = stream * width
        whole = in_ref[:, top : top + width].astype(F32)
        for sub in subs:
            data = whole[:, sub * lines : (sub + 1) * lines]
            data = data.reshape(blocks * lines, tok_rows).astype(BF16)
            outer[stream, sub] = jnp.dot(
                outer_ref[: 2 * back_rows],
                jnp.concatenate([data, data], axis=0),
                preferred_element_type=F32,
            )

    def twist(stream):
        for k in range(blocks + 1):
            halves = [[], []]
            turns = [(cos_ref[k : k + 1, at], sin_ref[k : k + 1, at]) for at in (first, second)]
            for sub in subs:
                twisted = []
                for cols, (cos, sin) in zip((first, second), turns):
                    re = outer[stream, sub, of_freq(k), cols]
                    if k == 0:
                        twisted.append((re, jnp.zeros_like(re)))
                        continue
                    if k == blocks:
                        twisted.append((re * cos, -(re * sin)))
                        continue
                    im = outer[stream, sub, of_freq(k - 1, real_rows), cols]
                    twisted.append((re * cos + im * sin, im * cos - re * sin))
                (re_a, im_a), (re_b, im_b) = twisted
                halves[0].append(jnp.concatenate([re_a + re_b, im_a + im_b], axis=1))
                halves[1].append(jnp.concatenate([re_a - re_b, im_a - im_b], axis=1))
            at = slice(k * width, (k + 1) * width)
            for parts, high, low in (
                (halves[0], even_high, even_low),
                (halves[1], odd_high, odd_low),
            ):
                joined = jnp.concatenate(parts, axis=0)
                high[stream, at], low[stream, at] = split_parts(joined)

    outer_dft(0)
    outer_dft(1)
    twist(0)
    sig_even = inner_dft(even_high[0], even_low[0], even_ref)
    sig_odd = inner_dft(odd_high[0], odd_low[0], odd_ref)
    twist(1)
    ker_even = inner_dft(even_high[1], even_low[1], even_ref)
    ker_odd = inner_dft(odd_high[1], odd_low[1], odd_ref)
    for sig, ker, back_table_ref, out in (
        (sig_even, ker_even, even_ref, even),
        (sig_odd, ker_odd, back_ref, odd),
    ):
        sig_re, sig_im = sig[:, first], sig[:, second]
        ker_re, ker_im = ker[:, first], ker[:, second]
        prod_re = sig_re * ker_re - sig_im * ker_im
        prod_neg = -(sig_re * ker_im + sig_im * ker_re)
        product = jnp.concatenate([prod_re, prod_neg], axis=1)
        out[...] = inner_dft(*split_parts(product), back_table_ref)

    for k in range(blocks + 1):
        for cols, sign in ((first, 1), (second, -1)):
            cos, sin = cos_ref[k : k + 1, cols], sin_ref[k : k + 1, cols]
            for sub in subs:
                at = slice(k * width + sub * lines, k * width + (sub + 1) * lines)
                z = even[at] + odd[at] if sign > 0 else even[at] - odd[at]
                re, neg = z[:, first], z[:, second]
                outer[0, sub, of_freq(k), cols] = re * cos + neg * sin
                if 0 < k < blocks:
                    outer[0, sub, of_freq(k - 1, real_rows), cols] = re * sin - neg * cos
    parts = []
    for sub in subs:
        high, low = split_parts(outer[0, sub])
        back = jnp.dot(high_ref[...], low, preferred_element_type=F32)
        back += jnp.dot(low_ref[...], high, preferred_element_type=F32)
        back += jnp.dot(high_ref[...], high, preferred_element_type=F32)
        parts.append(back.reshape(blocks, lines, tok_rows))
    out_ref[...] = jnp.concatenate(parts, axis=1).astype(BF16)


def gate_kernel(order_in, order_out, q_ref, conv_ref, out_ref):
    groups, width, tok_rows = conv_ref.shape
    parts = [conv_ref[order_in.index(group)].astype(F32) for group in range(groups)]
    convolved = jnp.concatenate(parts, axis=0).T
    gated_rows = (q_ref[...].astype(F32) * convolved).astype(BF16)
    tokens = out_ref.shape[1]
    for n, group in enumerate(order_out):
        out_ref[n] = gated_rows[group * tokens : (group + 1) * tokens]


def norm_kernel(order, rows_ref, gain_ref, out_ref):
    groups, _, width = rows_ref.shape
    squares = 0.0
    for n in range(groups):
        widened = rows_ref[n].astype(F32)
        squares = squares + widened * widened
    total = jnp.sum(squares, axis=1, keepdims=True)
    scaling = lax.rsqrt(total / (groups * width) + 1e-05)
    for n, group in enumerate(order):
        cols = slice(group * width, (group + 1) * width)
        row = rows_ref[n].astype(F32)
        out_ref[:, cols] = (row * scaling * gain_ref[:, cols]).astype(BF16)


def on_device(kernel, out_shape, cost, scratch=(), **specs):
    return pl.pallas_call(
        kernel,
        out_shape=out_shape,
        scratch_shapes=list(scratch),
        compiler_params=pltpu.CompilerParams(vmem_limit_bytes=VMEM_BYTES),
        cost_estimate=pl.CostEstimate(
            flops=cost[0], bytes_accessed=cost[1], transcendentals=0
        ),
        **specs,
    )


def mix(k_stream, v_stream, filters, order):
    tok_rows, channels = k_stream.shape
    groups = len(order)
    shape = jax.ShapeDtypeStruct((groups, 2 * channels // groups, tok_rows), BF16)
    cost = (k_stream.size, 12 * k_stream.size)
    scratch = [pltpu.VMEM(k_stream.shape, BF16)] * 2
    scratch += [pltpu.VMEM(k_stream.shape, F32), pltpu.SemaphoreType.DMA((4,))]
    specs = [pl.BlockSpec(memory_space=pltpu.HBM)] * 3
    held = [
        pltpu.with_memory_space_constraint(array, pltpu.HBM)
        for array in (k_stream, v_stream, filters)
    ]
    kernel = functools.partial(mix_kernel, order)
    return on_device(kernel, shape, cost, scratch, in_specs=specs)(*held)


def convolve(pieces, order_in, order_out):
    blocks, rows, tok_rows = pieces.shape
    width = rows // 2
    lines = 8
    tables = (
        np.stack(twist_tables(blocks, tok_rows)),
        np.stack(inner_tables(tok_rows)),
        np.concatenate(
            outer_tables(blocks, tok_rows, lines, order_in, order_out), axis=0
        ),
    )
    shape = jax.ShapeDtypeStruct((blocks, width, tok_rows), BF16)
    freq_rows = (blocks + 1) * width
    scratch = [pltpu.VMEM((2, width // lines, 2 * blocks * lines, tok_rows), F32)]
    scratch += [pltpu.VMEM((2, freq_rows, tok_rows), BF16)] * 4
    scratch += [pltpu.VMEM((freq_rows, tok_rows), F32)] * 2
    cost = (2 * 3 * freq_rows * 3 * 2 * tok_rows * tok_rows, 2 * 2**20)
    return on_device(conv_kernel, shape, cost, scratch)(
        pieces, *(jnp.asarray(table) for table in tables)
    )


def gate(q_stream, convolved, order_in, order_out):
    tok_rows, channels = q_stream.shape
    count = len(order_out)
    shape = jax.ShapeDtypeStruct((count, tok_rows // count, channels), BF16)
    cost = (q_stream.size, 6 * q_stream.size)
    kernel = functools.partial(gate_kernel, order_in, order_out)
    return on_device(kernel, shape, cost)(q_stream, convolved)


def normalize(rows, norm_gain, order):
    groups, tokens, width = rows.shape
    channels = groups * width
    shape = jax.ShapeDtypeStruct((tokens, channels), BF16)
    cost = (6 * tokens * channels, 4 * tokens * channels + 4 * channels)
    kernel = functools.partial(norm_kernel, order)
    return on_device(kernel, shape, cost)(rows, norm_gain.reshape(1, channels))


def exchange(array, axis, order):
    return lax.all_to_all(
        array, axis, split_axis=0, concat_axis=0, axis_index_groups=[order], tiled=True
    )


def spread(planes, lines, places):
    far = [0]
    while len(far) < planes:
        far = [2 * n for n in far] + [2 * n + 1 for n in far]
    first_to_last = [
        (plane * lines + (turn + n) % lines) * places + place
        for place in range(places)
        for turn in range(lines)
        for n, plane in enumerate(far)
    ]
    return first_to_last[::-1]


def local(q_stream, k_stream, v_stream, filters, norm_gain):
    ctx, ch = lax.axis_size("ctx"), lax.axis_size("ch")
    order_ctx = spread(ctx // 4, 2, 2)
    order_ch = spread(ch // 2, 2, 1)
    pieces = exchange(mix(k_stream, v_stream, filters, order_ctx), "ctx", order_ctx)
    convolved = convolve(pieces, order_ctx, order_ctx)
    returned = exchange(convolved, "ctx", order_ctx)
    gated_rows = gate(q_stream, returned, order_ctx, order_ch)
    regrouped = exchange(gated_rows, "ch", order_ch)
    return normalize(regrouped, norm_gain, order_ch)


def solution(mesh):
    return jax.shard_map(
        local,
        mesh=mesh,
        in_specs=(P("ctx", "ch"), P("ctx", "ch"), P("ctx", "ch"), P("ctx", "ch"), P()),
        out_specs=P(("ctx", "ch"), None),
        check_vma=False,
    )
```

profile of v0, /device:TPU:120, one launch (start us, length us, event | category | flops | bytes accessed | tf_op | source)
XLA Modules:
  0.0 66.8 jit_solution(5453177872912938858)
XLA Ops:
  0.0 0.0 copy-start.2
  0.0 1.5 %shard_map.82 = bf16[32,32,256]{2,1,0:T(8,128)(2,1)S(1)} custom-call(bf16[256,512]{1,0:T(8,128)(2,1)} %k_hbm.1, bf16[256,512]{1,0:T(8,128)(2,1)} %v_hbm.1, f32[256,512]{1,0:T(8,128)} %filters_hbm.1), custom_call_target="tpu_custom_call" | custom-call | flops 131072 | bytes 1572864 | tf_op jit(solution)/shard_map/pallas_call | solution.py:248
  1.5 0.0 copy-start.3
  1.5 0.0 copy-start.4
  1.5 25.6 %all_to_all.15.in_ref = bf16[32,32,256]{2,1,0:T(8,128)(2,1)S(1)} all-to-all(bf16[32,32,256]{2,1,0:T(8,128)(2,1)S(1)} %shard_map.82), channel_id=1, replica_groups={{464,240,336,112,400,176,272,48,496,208,368,80,432,144,304,16,448,224,3..., dimensions={0} | all-to-all | bytes 1048576 | tf_op jit(solution)/shard_map/all_to_all | solution.py:292
  27.1 0.0 copy-done.2
  27.1 0.0 copy-done.3
  27.1 0.0 copy-done.4
  27.1 2.8 %shard_map.83 = bf16[32,16,256]{2,1,0:T(8,128)(2,1)S(1)} custom-call(bf16[32,32,256]{2,1,0:T(8,128)(2,1)S(1)} %all_to_all.15.in_ref, f32[2,33,256]{2,1,0:T(8,128)S(1)} %copy-done.4, bf16[3,512,256]{2,1,0:T(8,128)(2,1)S(1)} %copy-done.3, bf16[1024,512]{1,0:T(8,128)(2,1)S(1)} %copy-done.2), custom_call_target="tpu_custom_call" | custom-call | flops 1245708288 | bytes 2097152 | tf_op jit(solution)/shard_map/pallas_call | solution.py:268
  30.0 0.0 copy-start
  30.0 15.3 %all_to_all.16.conv_ref = bf16[32,16,256]{2,1,0:T(8,128)(2,1)S(1)} all-to-all(bf16[32,16,256]{2,1,0:T(8,128)(2,1)S(1)} %shard_map.83), channel_id=1, replica_groups={{464,240,336,112,400,176,272,48,496,208,368,80,432,144,304,16,448,224,3..., dimensions={0} | all-to-all | bytes 524288 | tf_op jit(solution)/shard_map/all_to_all | solution.py:292
  45.3 0.0 copy-done
  45.3 0.1 shard_map.84
  45.4 0.0 copy-start.1
  45.4 20.4 %all_to_all.17.rows_ref = bf16[16,16,512]{2,1,0:T(8,128)(2,1)S(1)} all-to-all(bf16[16,16,512]{2,1,0:T(8,128)(2,1)S(1)} %shard_map.84), channel_id=1, replica_groups={{14,7,10,3,12,5,8,1,15,6,11,2,13,4,9,0},{30,23,26,19,28,21,24,17,31,22,..., dimensions={0} | all-to-all | bytes 524288 | tf_op jit(solution)/shard_map/all_to_all | solution.py:292
  65.9 0.0 copy-done.1
  65.9 0.9 %shard_map.85 = bf16[16,8192]{1,0:T(8,128)(2,1)} custom-call(bf16[16,16,512]{2,1,0:T(8,128)(2,1)S(1)} %all_to_all.17.rows_ref, f32[1,8192]{1,0:T(1,128)S(1)} %bitcast.1), custom_call_target="tpu_custom_call" | custom-call | flops 786432 | bytes 557056 | tf_op jit(solution)/shard_map/pallas_call | solution.py:288
Async XLA Ops:
  0.0 27.1 %copy-start.2 = (bf16[1024,512]{1,0:T(8,128)(2,1)S(1)}, bf16[1024,512]{1,0:T(8,128)(2,1)}, u32[]{:S(2)}) copy-start(bf16[1024,512]{1,0:T(8,128)(2,1)} %constant.8.clone.outer_ref) | copy-start | bytes 3145732
  1.5 25.6 %copy-start.3 = (bf16[3,512,256]{2,1,0:T(8,128)(2,1)S(1)}, bf16[3,512,256]{2,1,0:T(8,128)(2,1)}, u32[]{:S(2)}) copy-start(bf16[3,512,256]{2,1,0:T(8,128)(2,1)} %constant.7.clone.inner_ref) | copy-start | bytes 2359300
  1.5 25.6 %copy-start.4 = (f32[2,33,256]{2,1,0:T(8,128)S(1)}, f32[2,33,256]{2,1,0:T(8,128)}, u32[]{:S(2)}) copy-start(f32[2,33,256]{2,1,0:T(8,128)} %constant.6.clone.twist_ref) | copy-start | bytes 202756
  30.0 15.3 %copy-start = (bf16[256,512]{1,0:T(8,128)(2,1)S(1)}, bf16[256,512]{1,0:T(8,128)(2,1)}, u32[]{:S(2)}) copy-start(bf16[256,512]{1,0:T(8,128)(2,1)} %q_ref.1) | copy-start | bytes 786436
  45.4 20.5 %copy-start.1 = (f32[8192]{0:T(1024)S(1)}, f32[8192]{0:T(1024)}, u32[]{:S(2)}) copy-start(f32[8192]{0:T(1024)} %param.12) | copy-start | bytes 98308
where the time goes:
time: 67 us; the launch traced here: 66.8 us
  blocking collectives  61.4 us (92%)
  Pallas kernels  5.31 us (8%)
    all_to_all x3, blocking collectives, exchange(): lax.all_to_all(array, axis, split_axis=0, concat_axis=0, axis_index_group...  61.4 us
    pallas_call x1, Pallas kernels, convolve(): on_device(conv_kernel, shape, cost, scratch)  2.81 us
    pallas_call x1, Pallas kernels, mix(): return on_device(kernel, shape, cost, scratch, in_specs=specs)(*held)  1.5 us

commit v1 on v0

--- a/solution.py
+++ b/solution.py
@@ -310,7 +310,7 @@
 def local(q_stream, k_stream, v_stream, filters, norm_gain):
     ctx, ch = lax.axis_size("ctx"), lax.axis_size("ch")
     order_ctx = spread(ctx // 4, 2, 2)
-    order_ch = spread(ch // 2, 2, 1)
+    order_ch = spread(ch // 2, 1, 2)
     pieces = exchange(mix(k_stream, v_stream, filters, order_ctx), "ctx", order_ctx)
     convolved = convolve(pieces, order_ctx, order_ctx)
     returned = exchange(convolved, "ctx", order_ctx)

time: 67 us -> 65 us (0.970)
  the two profiles are of different devices: /device:TPU:120 before, /device:TPU:6 now
where the time goes in v1:
time: 65 us; the launch traced here: 64.5 us
  blocking collectives  59 us (91%)
  Pallas kernels  5.32 us (8%)
    all_to_all x3, blocking collectives, exchange(): lax.all_to_all(array, axis, split_axis=0, concat_axis=0, axis_index_group...  59 us
    pallas_call x1, Pallas kernels, convolve(): on_device(conv_kernel, shape, cost, scratch)  2.82 us
    pallas_call x1, Pallas kernels, mix(): return on_device(kernel, shape, cost, scratch, in_specs=specs)(*held)  1.5 us

profile of v1, /device:TPU:6, one launch (start us, length us, event | category | flops | bytes accessed | tf_op | source)
XLA Modules:
  0.0 64.5 jit_solution(13964025226143361357)
XLA Ops:
  0.0 0.0 copy-start.2
  0.0 1.5 %shard_map.82 = bf16[32,32,256]{2,1,0:T(8,128)(2,1)S(1)} custom-call(bf16[256,512]{1,0:T(8,128)(2,1)} %k_hbm.1, bf16[256,512]{1,0:T(8,128)(2,1)} %v_hbm.1, f32[256,512]{1,0:T(8,128)} %filters_hbm.1), custom_call_target="tpu_custom_call" | custom-call | flops 131072 | bytes 1572864 | tf_op jit(solution)/shard_map/pallas_call | solution.py:248
  1.5 0.0 copy-start.3
  1.5 0.0 copy-start.4
  1.5 25.4 %all_to_all.15.in_ref = bf16[32,32,256]{2,1,0:T(8,128)(2,1)S(1)} all-to-all(bf16[32,32,256]{2,1,0:T(8,128)(2,1)S(1)} %shard_map.82), channel_id=1, replica_groups={{464,240,336,112,400,176,272,48,496,208,368,80,432,144,304,16,448,224,3..., dimensions={0} | all-to-all | bytes 1048576 | tf_op jit(solution)/shard_map/all_to_all | solution.py:292
  26.9 0.0 copy-done.2
  26.9 0.0 copy-done.3
  26.9 0.0 copy-done.4
  26.9 2.8 %shard_map.83 = bf16[32,16,256]{2,1,0:T(8,128)(2,1)S(1)} custom-call(bf16[32,32,256]{2,1,0:T(8,128)(2,1)S(1)} %all_to_all.15.in_ref, f32[2,33,256]{2,1,0:T(8,128)S(1)} %copy-done.4, bf16[3,512,256]{2,1,0:T(8,128)(2,1)S(1)} %copy-done.3, bf16[1024,512]{1,0:T(8,128)(2,1)S(1)} %copy-done.2), custom_call_target="tpu_custom_call" | custom-call | flops 1245708288 | bytes 2097152 | tf_op jit(solution)/shard_map/pallas_call | solution.py:268
  29.8 0.0 copy-start
  29.8 15.1 %all_to_all.16.conv_ref = bf16[32,16,256]{2,1,0:T(8,128)(2,1)S(1)} all-to-all(bf16[32,16,256]{2,1,0:T(8,128)(2,1)S(1)} %shard_map.83), channel_id=1, replica_groups={{464,240,336,112,400,176,272,48,496,208,368,80,432,144,304,16,448,224,3..., dimensions={0} | all-to-all | bytes 524288 | tf_op jit(solution)/shard_map/all_to_all | solution.py:292
  44.9 0.0 copy-done
  44.9 0.1 shard_map.84
  45.1 0.0 copy-start.1
  45.1 18.5 %all_to_all.17.rows_ref = bf16[16,16,512]{2,1,0:T(8,128)(2,1)S(1)} all-to-all(bf16[16,16,512]{2,1,0:T(8,128)(2,1)S(1)} %shard_map.84), channel_id=1, replica_groups={{15,7,11,3,13,5,9,1,14,6,10,2,12,4,8,0},{31,23,27,19,29,21,25,17,30,22,..., dimensions={0} | all-to-all | bytes 524288 | tf_op jit(solution)/shard_map/all_to_all | solution.py:292
  63.6 0.0 copy-done.1
  63.6 0.9 %shard_map.85 = bf16[16,8192]{1,0:T(8,128)(2,1)} custom-call(bf16[16,16,512]{2,1,0:T(8,128)(2,1)S(1)} %all_to_all.17.rows_ref, f32[1,8192]{1,0:T(1,128)S(1)} %bitcast.1), custom_call_target="tpu_custom_call" | custom-call | flops 786432 | bytes 557056 | tf_op jit(solution)/shard_map/pallas_call | solution.py:288
Async XLA Ops:
  0.0 26.9 %copy-start.2 = (bf16[1024,512]{1,0:T(8,128)(2,1)S(1)}, bf16[1024,512]{1,0:T(8,128)(2,1)}, u32[]{:S(2)}) copy-start(bf16[1024,512]{1,0:T(8,128)(2,1)} %constant.8.clone.outer_ref) | copy-start | bytes 3145732
  1.5 25.4 %copy-start.3 = (bf16[3,512,256]{2,1,0:T(8,128)(2,1)S(1)}, bf16[3,512,256]{2,1,0:T(8,128)(2,1)}, u32[]{:S(2)}) copy-start(bf16[3,512,256]{2,1,0:T(8,128)(2,1)} %constant.7.clone.inner_ref) | copy-start | bytes 2359300
  1.5 25.4 %copy-start.4 = (f32[2,33,256]{2,1,0:T(8,128)S(1)}, f32[2,33,256]{2,1,0:T(8,128)}, u32[]{:S(2)}) copy-start(f32[2,33,256]{2,1,0:T(8,128)} %constant.6.clone.twist_ref) | copy-start | bytes 202756
  29.8 15.1 %copy-start = (bf16[256,512]{1,0:T(8,128)(2,1)S(1)}, bf16[256,512]{1,0:T(8,128)(2,1)}, u32[]{:S(2)}) copy-start(bf16[256,512]{1,0:T(8,128)(2,1)} %q_ref.1) | copy-start | bytes 786436
  45.1 18.5 %copy-start.1 = (f32[8192]{0:T(1024)S(1)}, f32[8192]{0:T(1024)}, u32[]{:S(2)}) copy-start(f32[8192]{0:T(1024)} %param.12) | copy-start | bytes 98308

commit v2 on v1

--- a/solution.py
+++ b/solution.py
@@ -294,23 +294,28 @@
     )
 
 
-def spread(planes, lines, places):
+def far_apart(count):
     far = [0]
-    while len(far) < planes:
+    while len(far) < count:
         far = [2 * n for n in far] + [2 * n + 1 for n in far]
-    first_to_last = [
-        (plane * lines + (turn + n) % lines) * places + place
-        for place in range(places)
-        for turn in range(lines)
-        for n, plane in enumerate(far)
-    ]
-    return first_to_last[::-1]
+    return far
+
+
+def listed(places):
+    return places[::-1]
 
 
 def local(q_stream, k_stream, v_stream, filters, norm_gain):
     ctx, ch = lax.axis_size("ctx"), lax.axis_size("ch")
-    order_ctx = spread(ctx // 4, 2, 2)
-    order_ch = spread(ch // 2, 1, 2)
+    order_ctx = listed(
+        [
+            z * 4 + (x + n) % 2 * 2 + core
+            for x in range(2)
+            for n, z in enumerate(far_apart(ctx // 4))
+            for core in range(2)
+        ]
+    )
+    order_ch = listed([y * 2 + x for x in range(2) for y in far_apart(ch // 2)])
     pieces = exchange(mix(k_stream, v_stream, filters, order_ctx), "ctx", order_ctx)
     convolved = convolve(pieces, order_ctx, order_ctx)
     returned = exchange(convolved, "ctx", order_ctx)

time: 65 us -> 65.7 us (1.011)
  blocking collectives: 59 us -> 60 us
    all_to_all x3, blocking collectives: 59 us -> 60 us  [exchange(): lax.all_to_all(array, axis, split_axis=0, concat_axis=0, axis_index_group...]
where the time goes in v2:
time: 65.7 us; the launch traced here: 65.4 us
  blocking collectives  60 us (91%)
  Pallas kernels  5.32 us (8%)
    all_to_all x3, blocking collectives, exchange(): lax.all_to_all(array, axis, split_axis=0, concat_axis=0, axis_index_group...  60 us
    pallas_call x1, Pallas kernels, convolve(): on_device(conv_kernel, shape, cost, scratch)  2.82 us
    pallas_call x1, Pallas kernels, mix(): return on_device(kernel, shape, cost, scratch, in_specs=specs)(*held)  1.5 us

profile of v2, /device:TPU:6, one launch (start us, length us, event | category | flops | bytes accessed | tf_op | source)
XLA Modules:
  0.0 65.4 jit_solution(15394983630665213333)
XLA Ops:
  0.0 0.0 copy-start.2
  0.0 1.5 %shard_map.82 = bf16[32,32,256]{2,1,0:T(8,128)(2,1)S(1)} custom-call(bf16[256,512]{1,0:T(8,128)(2,1)} %k_hbm.1, bf16[256,512]{1,0:T(8,128)(2,1)} %v_hbm.1, f32[256,512]{1,0:T(8,128)} %filters_hbm.1), custom_call_target="tpu_custom_call" | custom-call | flops 131072 | bytes 1572864 | tf_op jit(solution)/shard_map/pallas_call | solution.py:248
  1.5 0.0 copy-start.3
  1.5 0.0 copy-start.4
  1.5 25.3 %all_to_all.15.in_ref = bf16[32,32,256]{2,1,0:T(8,128)(2,1)S(1)} all-to-all(bf16[32,32,256]{2,1,0:T(8,128)(2,1)S(1)} %shard_map.82), channel_id=1, replica_groups={{464,448,240,224,336,320,112,96,400,384,176,160,272,256,48,32,496,480,2..., dimensions={0} | all-to-all | bytes 1048576 | tf_op jit(solution)/shard_map/all_to_all | solution.py:292
  26.8 0.0 copy-done.2
  26.8 0.0 copy-done.3
  26.8 0.0 copy-done.4
  26.8 2.8 %shard_map.83 = bf16[32,16,256]{2,1,0:T(8,128)(2,1)S(1)} custom-call(bf16[32,32,256]{2,1,0:T(8,128)(2,1)S(1)} %all_to_all.15.in_ref, f32[2,33,256]{2,1,0:T(8,128)S(1)} %copy-done.4, bf16[3,512,256]{2,1,0:T(8,128)(2,1)S(1)} %copy-done.3, bf16[1024,512]{1,0:T(8,128)(2,1)S(1)} %copy-done.2), custom_call_target="tpu_custom_call" | custom-call | flops 1245708288 | bytes 2097152 | tf_op jit(solution)/shard_map/pallas_call | solution.py:268
  29.7 0.0 copy-start
  29.7 16.3 %all_to_all.16.conv_ref = bf16[32,16,256]{2,1,0:T(8,128)(2,1)S(1)} all-to-all(bf16[32,16,256]{2,1,0:T(8,128)(2,1)S(1)} %shard_map.83), channel_id=1, replica_groups={{464,448,240,224,336,320,112,96,400,384,176,160,272,256,48,32,496,480,2..., dimensions={0} | all-to-all | bytes 524288 | tf_op jit(solution)/shard_map/all_to_all | solution.py:292
  46.0 0.0 copy-done
  46.0 0.1 shard_map.84
  46.1 0.0 copy-start.1
  46.1 18.4 %all_to_all.17.rows_ref = bf16[16,16,512]{2,1,0:T(8,128)(2,1)S(1)} all-to-all(bf16[16,16,512]{2,1,0:T(8,128)(2,1)S(1)} %shard_map.84), channel_id=1, replica_groups={{15,7,11,3,13,5,9,1,14,6,10,2,12,4,8,0},{31,23,27,19,29,21,25,17,30,22,..., dimensions={0} | all-to-all | bytes 524288 | tf_op jit(solution)/shard_map/all_to_all | solution.py:292
  64.5 0.0 copy-done.1
  64.5 0.9 %shard_map.85 = bf16[16,8192]{1,0:T(8,128)(2,1)} custom-call(bf16[16,16,512]{2,1,0:T(8,128)(2,1)S(1)} %all_to_all.17.rows_ref, f32[1,8192]{1,0:T(1,128)S(1)} %bitcast.1), custom_call_target="tpu_custom_call" | custom-call | flops 786432 | bytes 557056 | tf_op jit(solution)/shard_map/pallas_call | solution.py:288
Async XLA Ops:
  0.0 26.8 %copy-start.2 = (bf16[1024,512]{1,0:T(8,128)(2,1)S(1)}, bf16[1024,512]{1,0:T(8,128)(2,1)}, u32[]{:S(2)}) copy-start(bf16[1024,512]{1,0:T(8,128)(2,1)} %constant.8.clone.outer_ref) | copy-start | bytes 3145732
  1.5 25.3 %copy-start.3 = (bf16[3,512,256]{2,1,0:T(8,128)(2,1)S(1)}, bf16[3,512,256]{2,1,0:T(8,128)(2,1)}, u32[]{:S(2)}) copy-start(bf16[3,512,256]{2,1,0:T(8,128)(2,1)} %constant.7.clone.inner_ref) | copy-start | bytes 2359300
  1.5 25.3 %copy-start.4 = (f32[2,33,256]{2,1,0:T(8,128)S(1)}, f32[2,33,256]{2,1,0:T(8,128)}, u32[]{:S(2)}) copy-start(f32[2,33,256]{2,1,0:T(8,128)} %constant.6.clone.twist_ref) | copy-start | bytes 202756
  29.7 16.3 %copy-start = (bf16[256,512]{1,0:T(8,128)(2,1)S(1)}, bf16[256,512]{1,0:T(8,128)(2,1)}, u32[]{:S(2)}) copy-start(bf16[256,512]{1,0:T(8,128)(2,1)} %q_ref.1) | copy-start | bytes 786436
  46.1 18.4 %copy-start.1 = (f32[8192]{0:T(1024)S(1)}, f32[8192]{0:T(1024)}, u32[]{:S(2)}) copy-start(f32[8192]{0:T(1024)} %param.12) | copy-start | bytes 98308

commit v3 on v2

--- a/solution.py
+++ b/solution.py
@@ -307,7 +307,7 @@
 
 def local(q_stream, k_stream, v_stream, filters, norm_gain):
     ctx, ch = lax.axis_size("ctx"), lax.axis_size("ch")
-    order_ctx = listed(
+    order_in = listed(
         [
             z * 4 + (x + n) % 2 * 2 + core
             for x in range(2)
@@ -315,11 +315,19 @@
             for core in range(2)
         ]
     )
+    order_back = listed(
+        [
+            z * 4 + (x + n) % 2 * 2 + core
+            for core in range(2)
+            for x in range(2)
+            for n, z in enumerate(far_apart(ctx // 4))
+        ]
+    )
     order_ch = listed([y * 2 + x for x in range(2) for y in far_apart(ch // 2)])
-    pieces = exchange(mix(k_stream, v_stream, filters, order_ctx), "ctx", order_ctx)
-    convolved = convolve(pieces, order_ctx, order_ctx)
-    returned = exchange(convolved, "ctx", order_ctx)
-    gated_rows = gate(q_stream, returned, order_ctx, order_ch)
+    pieces = exchange(mix(k_stream, v_stream, filters, order_in), "ctx", order_in)
+    convolved = convolve(pieces, order_in, order_back)
+    returned = exchange(convolved, "ctx", order_back)
+    gated_rows = gate(q_stream, returned, order_back, order_ch)
     regrouped = exchange(gated_rows, "ch", order_ch)
     return normalize(regrouped, norm_gain, order_ch)
 

time: 65.7 us -> 65.2 us (level)
  blocking collectives: 60 us -> 59.1 us
    all_to_all x3, blocking collectives: 60 us -> 59.1 us  [exchange(): lax.all_to_all(array, axis, split_axis=0, concat_axis=0, axis_index_group...]
where the time goes in v3:
time: 65.2 us; the launch traced here: 64.5 us
  blocking collectives  59.1 us (91%)
  Pallas kernels  5.32 us (8%)
    all_to_all x3, blocking collectives, exchange(): lax.all_to_all(array, axis, split_axis=0, concat_axis=0, axis_index_group...  59.1 us
    pallas_call x1, Pallas kernels, convolve(): on_device(conv_kernel, shape, cost, scratch)  2.82 us
    pallas_call x1, Pallas kernels, mix(): return on_device(kernel, shape, cost, scratch, in_specs=specs)(*held)  1.5 us

profile of v3, /device:TPU:6, one launch (start us, length us, event | category | flops | bytes accessed | tf_op | source)
XLA Modules:
  0.0 64.5 jit_solution(3334003196657930627)
XLA Ops:
  0.0 0.0 copy-start.2
  0.0 1.5 %shard_map.82 = bf16[32,32,256]{2,1,0:T(8,128)(2,1)S(1)} custom-call(bf16[256,512]{1,0:T(8,128)(2,1)} %k_hbm.1, bf16[256,512]{1,0:T(8,128)(2,1)} %v_hbm.1, f32[256,512]{1,0:T(8,128)} %filters_hbm.1), custom_call_target="tpu_custom_call" | custom-call | flops 131072 | bytes 1572864 | tf_op jit(solution)/shard_map/pallas_call | solution.py:248
  1.5 0.0 copy-start.3
  1.5 0.0 copy-start.4
  1.5 25.3 %all_to_all.15.in_ref = bf16[32,32,256]{2,1,0:T(8,128)(2,1)S(1)} all-to-all(bf16[32,32,256]{2,1,0:T(8,128)(2,1)S(1)} %shard_map.82), channel_id=1, replica_groups={{464,448,240,224,336,320,112,96,400,384,176,160,272,256,48,32,496,480,2..., dimensions={0} | all-to-all | bytes 1048576 | tf_op jit(solution)/shard_map/all_to_all | solution.py:292
  26.8 0.0 copy-done.2
  26.8 0.0 copy-done.3
  26.8 0.0 copy-done.4
  26.8 2.8 %shard_map.83 = bf16[32,16,256]{2,1,0:T(8,128)(2,1)S(1)} custom-call(bf16[32,32,256]{2,1,0:T(8,128)(2,1)S(1)} %all_to_all.15.in_ref, f32[2,33,256]{2,1,0:T(8,128)S(1)} %copy-done.4, bf16[3,512,256]{2,1,0:T(8,128)(2,1)S(1)} %copy-done.3, bf16[1024,512]{1,0:T(8,128)(2,1)S(1)} %copy-done.2), custom_call_target="tpu_custom_call" | custom-call | flops 1245708288 | bytes 2097152 | tf_op jit(solution)/shard_map/pallas_call | solution.py:268
  29.7 0.0 copy-start
  29.7 15.4 %all_to_all.16.conv_ref = bf16[32,16,256]{2,1,0:T(8,128)(2,1)S(1)} all-to-all(bf16[32,16,256]{2,1,0:T(8,128)(2,1)S(1)} %shard_map.83), channel_id=1, replica_groups={{464,240,336,112,400,176,272,48,496,208,368,80,432,144,304,16,448,224,3..., dimensions={0} | all-to-all | bytes 524288 | tf_op jit(solution)/shard_map/all_to_all | solution.py:292
  45.1 0.0 copy-done
  45.1 0.1 shard_map.84
  45.2 0.0 copy-start.1
  45.2 18.4 %all_to_all.17.rows_ref = bf16[16,16,512]{2,1,0:T(8,128)(2,1)S(1)} all-to-all(bf16[16,16,512]{2,1,0:T(8,128)(2,1)S(1)} %shard_map.84), channel_id=1, replica_groups={{15,7,11,3,13,5,9,1,14,6,10,2,12,4,8,0},{31,23,27,19,29,21,25,17,30,22,..., dimensions={0} | all-to-all | bytes 524288 | tf_op jit(solution)/shard_map/all_to_all | solution.py:292
  63.7 0.0 copy-done.1
  63.7 0.9 %shard_map.85 = bf16[16,8192]{1,0:T(8,128)(2,1)} custom-call(bf16[16,16,512]{2,1,0:T(8,128)(2,1)S(1)} %all_to_all.17.rows_ref, f32[1,8192]{1,0:T(1,128)S(1)} %bitcast.1), custom_call_target="tpu_custom_call" | custom-call | flops 786432 | bytes 557056 | tf_op jit(solution)/shard_map/pallas_call | solution.py:288
Async XLA Ops:
  0.0 26.8 %copy-start.2 = (bf16[1024,512]{1,0:T(8,128)(2,1)S(1)}, bf16[1024,512]{1,0:T(8,128)(2,1)}, u32[]{:S(2)}) copy-start(bf16[1024,512]{1,0:T(8,128)(2,1)} %constant.8.clone.outer_ref) | copy-start | bytes 3145732
  1.5 25.3 %copy-start.3 = (bf16[3,512,256]{2,1,0:T(8,128)(2,1)S(1)}, bf16[3,512,256]{2,1,0:T(8,128)(2,1)}, u32[]{:S(2)}) copy-start(bf16[3,512,256]{2,1,0:T(8,128)(2,1)} %constant.7.clone.inner_ref) | copy-start | bytes 2359300
  1.5 25.3 %copy-start.4 = (f32[2,33,256]{2,1,0:T(8,128)S(1)}, f32[2,33,256]{2,1,0:T(8,128)}, u32[]{:S(2)}) copy-start(f32[2,33,256]{2,1,0:T(8,128)} %constant.6.clone.twist_ref) | copy-start | bytes 202756
  29.7 15.4 %copy-start = (bf16[256,512]{1,0:T(8,128)(2,1)S(1)}, bf16[256,512]{1,0:T(8,128)(2,1)}, u32[]{:S(2)}) copy-start(bf16[256,512]{1,0:T(8,128)(2,1)} %q_ref.1) | copy-start | bytes 786436
  45.2 18.4 %copy-start.1 = (f32[8192]{0:T(1024)S(1)}, f32[8192]{0:T(1024)}, u32[]{:S(2)}) copy-start(f32[8192]{0:T(1024)} %param.12) | copy-start | bytes 98308

commit v4 on v3

--- a/solution.py
+++ b/solution.py
@@ -309,9 +309,9 @@
     ctx, ch = lax.axis_size("ctx"), lax.axis_size("ch")
     order_in = listed(
         [
-            z * 4 + (x + n) % 2 * 2 + core
+            z * 4 + (x + z) % 2 * 2 + core
             for x in range(2)
-            for n, z in enumerate(far_apart(ctx // 4))
+            for z in range(ctx // 4)
             for core in range(2)
         ]
     )
@@ -323,7 +323,8 @@
             for n, z in enumerate(far_apart(ctx // 4))
         ]
     )
-    order_ch = listed([y * 2 + x for x in range(2) for y in far_apart(ch // 2)])
+    by_start = sorted(range(ch), key=lambda n: n // 2 + 4.6 * (n % 2))
+    order_ch = listed(by_start)
     pieces = exchange(mix(k_stream, v_stream, filters, order_in), "ctx", order_in)
     convolved = convolve(pieces, order_in, order_back)
     returned = exchange(convolved, "ctx", order_back)

time: 65.2 us -> 65.9 us (1.011)
  the two profiles are of different devices: /device:TPU:6 before, /device:TPU:64 now
where the time goes in v4:
time: 65.9 us; the launch traced here: 65.6 us
  blocking collectives  60.2 us (91%)
  Pallas kernels  5.32 us (8%)
    all_to_all x3, blocking collectives, exchange(): lax.all_to_all(array, axis, split_axis=0, concat_axis=0, axis_index_group...  60.2 us
    pallas_call x1, Pallas kernels, convolve(): on_device(conv_kernel, shape, cost, scratch)  2.82 us
    pallas_call x1, Pallas kernels, mix(): return on_device(kernel, shape, cost, scratch, in_specs=specs)(*held)  1.5 us

profile of v4, /device:TPU:64, one launch (start us, length us, event | category | flops | bytes accessed | tf_op | source)
XLA Modules:
  0.0 65.6 jit_solution(12718608994191302134)
XLA Ops:
  0.0 0.0 copy-start.2
  0.0 1.5 %shard_map.82 = bf16[32,32,256]{2,1,0:T(8,128)(2,1)S(1)} custom-call(bf16[256,512]{1,0:T(8,128)(2,1)} %k_hbm.1, bf16[256,512]{1,0:T(8,128)(2,1)} %v_hbm.1, f32[256,512]{1,0:T(8,128)} %filters_hbm.1), custom_call_target="tpu_custom_call" | custom-call | flops 131072 | bytes 1572864 | tf_op jit(solution)/shard_map/pallas_call | solution.py:248
  1.5 0.0 copy-start.3
  1.5 0.0 copy-start.4
  1.5 24.8 %all_to_all.15.in_ref = bf16[32,32,256]{2,1,0:T(8,128)(2,1)S(1)} all-to-all(bf16[32,32,256]{2,1,0:T(8,128)(2,1)S(1)} %shard_map.82), channel_id=1, replica_groups={{464,448,432,416,336,320,304,288,208,192,176,160,80,64,48,32,496,480,40..., dimensions={0} | all-to-all | bytes 1048576 | tf_op jit(solution)/shard_map/all_to_all | solution.py:292
  26.4 0.0 copy-done.2
  26.4 0.0 copy-done.3
  26.4 0.0 copy-done.4
  26.4 2.8 %shard_map.83 = bf16[32,16,256]{2,1,0:T(8,128)(2,1)S(1)} custom-call(bf16[32,32,256]{2,1,0:T(8,128)(2,1)S(1)} %all_to_all.15.in_ref, f32[2,33,256]{2,1,0:T(8,128)S(1)} %copy-done.4, bf16[3,512,256]{2,1,0:T(8,128)(2,1)S(1)} %copy-done.3, bf16[1024,512]{1,0:T(8,128)(2,1)S(1)} %copy-done.2), custom_call_target="tpu_custom_call" | custom-call | flops 1245708288 | bytes 2097152 | tf_op jit(solution)/shard_map/pallas_call | solution.py:268
  29.2 0.0 copy-start
  29.2 16.1 %all_to_all.16.conv_ref = bf16[32,16,256]{2,1,0:T(8,128)(2,1)S(1)} all-to-all(bf16[32,16,256]{2,1,0:T(8,128)(2,1)S(1)} %shard_map.83), channel_id=1, replica_groups={{464,240,336,112,400,176,272,48,496,208,368,80,432,144,304,16,448,224,3..., dimensions={0} | all-to-all | bytes 524288 | tf_op jit(solution)/shard_map/all_to_all | solution.py:292
  45.3 0.0 copy-done
  45.3 0.1 shard_map.84
  45.5 0.0 copy-start.1
  45.5 19.3 %all_to_all.17.rows_ref = bf16[16,16,512]{2,1,0:T(8,128)(2,1)S(1)} all-to-all(bf16[16,16,512]{2,1,0:T(8,128)(2,1)S(1)} %shard_map.84), channel_id=1, replica_groups={{15,13,11,9,7,14,5,12,3,10,1,8,6,4,2,0},{31,29,27,25,23,30,21,28,19,26,..., dimensions={0} | all-to-all | bytes 524288 | tf_op jit(solution)/shard_map/all_to_all | solution.py:292
  64.8 0.0 copy-done.1
  64.8 0.9 %shard_map.85 = bf16[16,8192]{1,0:T(8,128)(2,1)} custom-call(bf16[16,16,512]{2,1,0:T(8,128)(2,1)S(1)} %all_to_all.17.rows_ref, f32[1,8192]{1,0:T(1,128)S(1)} %bitcast.1), custom_call_target="tpu_custom_call" | custom-call | flops 786432 | bytes 557056 | tf_op jit(solution)/shard_map/pallas_call | solution.py:288
Async XLA Ops:
  0.0 26.4 %copy-start.2 = (bf16[1024,512]{1,0:T(8,128)(2,1)S(1)}, bf16[1024,512]{1,0:T(8,128)(2,1)}, u32[]{:S(2)}) copy-start(bf16[1024,512]{1,0:T(8,128)(2,1)} %constant.8.clone.outer_ref) | copy-start | bytes 3145732
  1.5 24.9 %copy-start.3 = (bf16[3,512,256]{2,1,0:T(8,128)(2,1)S(1)}, bf16[3,512,256]{2,1,0:T(8,128)(2,1)}, u32[]{:S(2)}) copy-start(bf16[3,512,256]{2,1,0:T(8,128)(2,1)} %constant.7.clone.inner_ref) | copy-start | bytes 2359300
  1.5 24.8 %copy-start.4 = (f32[2,33,256]{2,1,0:T(8,128)S(1)}, f32[2,33,256]{2,1,0:T(8,128)}, u32[]{:S(2)}) copy-start(f32[2,33,256]{2,1,0:T(8,128)} %constant.6.clone.twist_ref) | copy-start | bytes 202756
  29.2 16.1 %copy-start = (bf16[256,512]{1,0:T(8,128)(2,1)S(1)}, bf16[256,512]{1,0:T(8,128)(2,1)}, u32[]{:S(2)}) copy-start(bf16[256,512]{1,0:T(8,128)(2,1)} %q_ref.1) | copy-start | bytes 786436
  45.5 19.3 %copy-start.1 = (f32[8192]{0:T(1024)S(1)}, f32[8192]{0:T(1024)}, u32[]{:S(2)}) copy-start(f32[8192]{0:T(1024)} %param.12) | copy-start | bytes 98308

commit v5 on v3

--- a/solution.py
+++ b/solution.py
@@ -74,13 +74,13 @@
         copy.start()
     copies[0].wait()
     copies[1].wait()
-    mixed = (k_ref[...].astype(F32) * v_ref[...].astype(F32)).T
-    mixed = mixed.reshape(groups, width, tok_rows).astype(BF16)
+    mixed = (k_ref[...].astype(F32) * v_ref[...].astype(F32)).astype(BF16)
+    mixed = mixed.T.reshape(groups, width, tok_rows)
     for n, group in enumerate(order):
         out_ref[n, :width] = mixed[group]
     for at, copy in zip(halves, copies[2:]):
         copy.wait()
-        taps = filters_ref[at].T.reshape(groups, width, half).astype(BF16)
+        taps = filters_ref[at].astype(BF16).T.reshape(groups, width, half)
         for n, group in enumerate(order):
             out_ref[n, width:, at] = taps[group]
 
@@ -91,10 +91,26 @@
 
 
 def inner_dft(high, low, table_ref):
-    left = jnp.concatenate([high, low, high], axis=1)
-    table = table_ref[...]
-    right = jnp.concatenate([table[: high.shape[1]], table], axis=0)
-    return jnp.dot(left, right, preferred_element_type=F32)
+    rows = high.shape[1]
+    table_high, table_low = table_ref[:rows], table_ref[rows:]
+    total = jnp.dot(high, table_low, preferred_element_type=F32)
+    yield total
+    total = total + jnp.dot(low, table_high, preferred_element_type=F32)
+    yield total
+    yield total + jnp.dot(high, table_high, preferred_element_type=F32)
+
+
+def side_by_side(matmuls, others):
+    steps = 3 * len(matmuls)
+    done, results = 0, []
+    for n, matmul in enumerate(matmuls):
+        for m, result in enumerate(matmul):
+            upto = len(others) * (3 * n + m + 1) // steps
+            for other in others[done:upto]:
+                other()
+            done = upto
+        results.append(result)
+    return results
 
 
 def conv_kernel(
@@ -129,51 +145,65 @@
                 preferred_element_type=F32,
             )
 
-    def twist(stream):
-        for k in range(blocks + 1):
-            halves = [[], []]
-            turns = [(cos_ref[k : k + 1, at], sin_ref[k : k + 1, at]) for at in (first, second)]
-            for sub in subs:
-                twisted = []
-                for cols, (cos, sin) in zip((first, second), turns):
-                    re = outer[stream, sub, of_freq(k), cols]
-                    if k == 0:
-                        twisted.append((re, jnp.zeros_like(re)))
-                        continue
-                    if k == blocks:
-                        twisted.append((re * cos, -(re * sin)))
-                        continue
-                    im = outer[stream, sub, of_freq(k - 1, real_rows), cols]
-                    twisted.append((re * cos + im * sin, im * cos - re * sin))
-                (re_a, im_a), (re_b, im_b) = twisted
-                halves[0].append(jnp.concatenate([re_a + re_b, im_a + im_b], axis=1))
-                halves[1].append(jnp.concatenate([re_a - re_b, im_a - im_b], axis=1))
-            at = slice(k * width, (k + 1) * width)
-            for parts, high, low in (
-                (halves[0], even_high, even_low),
-                (halves[1], odd_high, odd_low),
-            ):
-                joined = jnp.concatenate(parts, axis=0)
-                high[stream, at], low[stream, at] = split_parts(joined)
-
-    outer_dft(0)
-    outer_dft(1)
-    twist(0)
-    sig_even = inner_dft(even_high[0], even_low[0], even_ref)
-    sig_odd = inner_dft(odd_high[0], odd_low[0], odd_ref)
-    twist(1)
-    ker_even = inner_dft(even_high[1], even_low[1], even_ref)
-    ker_odd = inner_dft(odd_high[1], odd_low[1], odd_ref)
-    for sig, ker, back_table_ref, out in (
-        (sig_even, ker_even, even_ref, even),
-        (sig_odd, ker_odd, back_ref, odd),
-    ):
+    def twist(stream, k):
+        halves = [[], []]
+        turns = [(cos_ref[k : k + 1, at], sin_ref[k : k + 1, at]) for at in (first, second)]
+        for sub in subs:
+            twisted = []
+            for cols, (cos, sin) in zip((first, second), turns):
+                re = outer[stream, sub, of_freq(k), cols]
+                if k == 0:
+                    twisted.append((re, jnp.zeros_like(re)))
+                    continue
+                if k == blocks:
+                    twisted.append((re * cos, -(re * sin)))
+                    continue
+                im = outer[stream, sub, of_freq(k - 1, real_rows), cols]
+                twisted.append((re * cos + im * sin, im * cos - re * sin))
+            (re_a, im_a), (re_b, im_b) = twisted
+            halves[0].append(jnp.concatenate([re_a + re_b, im_a + im_b], axis=1))
+            halves[1].append(jnp.concatenate([re_a - re_b, im_a - im_b], axis=1))
+        at = slice(k * width, (k + 1) * width)
+        for parts, high, low in (
+            (halves[0], even_high, even_low),
+            (halves[1], odd_high, odd_low),
+        ):
+            joined = jnp.concatenate(parts, axis=0)
+            high[stream, at], low[stream, at] = split_parts(joined)
+
+    def product(sig, ker):
         sig_re, sig_im = sig[:, first], sig[:, second]
         ker_re, ker_im = ker[:, first], ker[:, second]
         prod_re = sig_re * ker_re - sig_im * ker_im
         prod_neg = -(sig_re * ker_im + sig_im * ker_re)
-        product = jnp.concatenate([prod_re, prod_neg], axis=1)
-        out[...] = inner_dft(*split_parts(product), back_table_ref)
+        return split_parts(jnp.concatenate([prod_re, prod_neg], axis=1))
+
+    outer_dft(0)
+    outer_dft(1)
+    for k in range(blocks + 1):
+        twist(0, k)
+    sig_even, sig_odd = side_by_side(
+        [
+            inner_dft(even_high[0], even_low[0], even_ref),
+            inner_dft(odd_high[0], odd_low[0], odd_ref),
+        ],
+        [functools.partial(twist, 1, k) for k in range(blocks + 1)],
+    )
+    made = {}
+
+    def make(name, sig, ker):
+        made[name] = product(sig, ker)
+
+    (ker_even,) = side_by_side([inner_dft(even_high[1], even_low[1], even_ref)], [])
+    (ker_odd,) = side_by_side(
+        [inner_dft(odd_high[1], odd_low[1], odd_ref)],
+        [functools.partial(make, "even", sig_even, ker_even)],
+    )
+    (even[...],) = side_by_side(
+        [inner_dft(*made["even"], even_ref)],
+        [functools.partial(make, "odd", sig_odd, ker_odd)],
+    )
+    (odd[...],) = side_by_side([inner_dft(*made["odd"], back_ref)], [])
 
     for k in range(blocks + 1):
         for cols, sign in ((first, 1), (second, -1)):
@@ -197,8 +227,8 @@
 
 def gate_kernel(order_in, order_out, q_ref, conv_ref, out_ref):
     groups, width, tok_rows = conv_ref.shape
-    parts = [conv_ref[order_in.index(group)].astype(F32) for group in range(groups)]
-    convolved = jnp.concatenate(parts, axis=0).T
+    parts = [conv_ref[order_in.index(group)] for group in range(groups)]
+    convolved = jnp.concatenate(parts, axis=0).T.astype(F32)
     gated_rows = (q_ref[...].astype(F32) * convolved).astype(BF16)
     tokens = out_ref.shape[1]
     for n, group in enumerate(order_out):

time: 65.2 us -> 65.1 us (level)
  no operation moved by 1% of the time
where the time goes in v5:
time: 65.1 us; the launch traced here: 64.4 us
  blocking collectives  59.1 us (91%)
  Pallas kernels  5.22 us (8%)
    all_to_all x3, blocking collectives, exchange(): lax.all_to_all(array, axis, split_axis=0, concat_axis=0, axis_index_group...  59.1 us
    pallas_call x1, Pallas kernels, convolve(): on_device(conv_kernel, shape, cost, scratch)  2.77 us
    pallas_call x1, Pallas kernels, mix(): return on_device(kernel, shape, cost, scratch, in_specs=specs)(*held)  1.46 us

profile of v5, /device:TPU:6, one launch (start us, length us, event | category | flops | bytes accessed | tf_op | source)
XLA Modules:
  0.0 64.4 jit_solution(14656483531522727981)
XLA Ops:
  0.0 0.0 copy-start.2
  0.0 1.5 %shard_map.82 = bf16[32,32,256]{2,1,0:T(8,128)(2,1)S(1)} custom-call(bf16[256,512]{1,0:T(8,128)(2,1)} %k_hbm.1, bf16[256,512]{1,0:T(8,128)(2,1)} %v_hbm.1, f32[256,512]{1,0:T(8,128)} %filters_hbm.1), custom_call_target="tpu_custom_call" | custom-call | flops 131072 | bytes 1572864 | tf_op jit(solution)/shard_map/pallas_call | solution.py:278
  1.5 0.0 copy-start.3
  1.5 0.0 copy-start.4
  1.5 25.3 %all_to_all.15.in_ref = bf16[32,32,256]{2,1,0:T(8,128)(2,1)S(1)} all-to-all(bf16[32,32,256]{2,1,0:T(8,128)(2,1)S(1)} %shard_map.82), channel_id=1, replica_groups={{464,448,240,224,336,320,112,96,400,384,176,160,272,256,48,32,496,480,2..., dimensions={0} | all-to-all | bytes 1048576 | tf_op jit(solution)/shard_map/all_to_all | solution.py:322
  26.8 0.0 copy-done.2
  26.8 0.0 copy-done.3
  26.8 0.0 copy-done.4
  26.8 2.8 %shard_map.83 = bf16[32,16,256]{2,1,0:T(8,128)(2,1)S(1)} custom-call(bf16[32,32,256]{2,1,0:T(8,128)(2,1)S(1)} %all_to_all.15.in_ref, f32[2,33,256]{2,1,0:T(8,128)S(1)} %copy-done.4, bf16[3,512,256]{2,1,0:T(8,128)(2,1)S(1)} %copy-done.3, bf16[1024,512]{1,0:T(8,128)(2,1)S(1)} %copy-done.2), custom_call_target="tpu_custom_call" | custom-call | flops 1245708288 | bytes 2097152 | tf_op jit(solution)/shard_map/pallas_call | solution.py:298
  29.6 0.0 copy-start
  29.6 15.4 %all_to_all.16.conv_ref = bf16[32,16,256]{2,1,0:T(8,128)(2,1)S(1)} all-to-all(bf16[32,16,256]{2,1,0:T(8,128)(2,1)S(1)} %shard_map.83), channel_id=1, replica_groups={{464,240,336,112,400,176,272,48,496,208,368,80,432,144,304,16,448,224,3..., dimensions={0} | all-to-all | bytes 524288 | tf_op jit(solution)/shard_map/all_to_all | solution.py:322
  45.0 0.0 copy-done
  45.0 0.1 shard_map.84
  45.1 0.0 copy-start.1
  45.1 18.4 %all_to_all.17.rows_ref = bf16[16,16,512]{2,1,0:T(8,128)(2,1)S(1)} all-to-all(bf16[16,16,512]{2,1,0:T(8,128)(2,1)S(1)} %shard_map.84), channel_id=1, replica_groups={{15,7,11,3,13,5,9,1,14,6,10,2,12,4,8,0},{31,23,27,19,29,21,25,17,30,22,..., dimensions={0} | all-to-all | bytes 524288 | tf_op jit(solution)/shard_map/all_to_all | solution.py:322
  63.5 0.0 copy-done.1
  63.5 0.9 %shard_map.85 = bf16[16,8192]{1,0:T(8,128)(2,1)} custom-call(bf16[16,16,512]{2,1,0:T(8,128)(2,1)S(1)} %all_to_all.17.rows_ref, f32[1,8192]{1,0:T(1,128)S(1)} %bitcast.1), custom_call_target="tpu_custom_call" | custom-call | flops 786432 | bytes 557056 | tf_op jit(solution)/shard_map/pallas_call | solution.py:318
Async XLA Ops:
  0.0 26.8 %copy-start.2 = (bf16[1024,512]{1,0:T(8,128)(2,1)S(1)}, bf16[1024,512]{1,0:T(8,128)(2,1)}, u32[]{:S(2)}) copy-start(bf16[1024,512]{1,0:T(8,128)(2,1)} %constant.8.clone.outer_ref) | copy-start | bytes 3145732
  1.5 25.3 %copy-start.3 = (bf16[3,512,256]{2,1,0:T(8,128)(2,1)S(1)}, bf16[3,512,256]{2,1,0:T(8,128)(2,1)}, u32[]{:S(2)}) copy-start(bf16[3,512,256]{2,1,0:T(8,128)(2,1)} %constant.7.clone.inner_ref) | copy-start | bytes 2359300
  1.5 25.3 %copy-start.4 = (f32[2,33,256]{2,1,0:T(8,128)S(1)}, f32[2,33,256]{2,1,0:T(8,128)}, u32[]{:S(2)}) copy-start(f32[2,33,256]{2,1,0:T(8,128)} %constant.6.clone.twist_ref) | copy-start | bytes 202756
  29.6 15.4 %copy-start = (bf16[256,512]{1,0:T(8,128)(2,1)S(1)}, bf16[256,512]{1,0:T(8,128)(2,1)}, u32[]{:S(2)}) copy-start(bf16[256,512]{1,0:T(8,128)(2,1)} %q_ref.1) | copy-start | bytes 786436
  45.1 18.4 %copy-start.1 = (f32[8192]{0:T(1024)S(1)}, f32[8192]{0:T(1024)}, u32[]{:S(2)}) copy-start(f32[8192]{0:T(1024)} %param.12) | copy-start | bytes 98308

commit v6 on v5

--- a/solution.py
+++ b/solution.py
@@ -325,10 +325,7 @@
 
 
 def far_apart(count):
-    far = [0]
-    while len(far) < count:
-        far = [2 * n for n in far] + [2 * n + 1 for n in far]
-    return far
+    return [(n + 1) // 2 if n % 2 else -n // 2 % count for n in range(count)]
 
 
 def listed(places):

time: 65.1 us -> 66.8 us (1.026)
  the two profiles are of different devices: /device:TPU:6 before, /device:TPU:1 now
where the time goes in v6:
time: 66.8 us; the launch traced here: 66.5 us
  blocking collectives  61.2 us (92%)
  Pallas kernels  5.22 us (8%)
    all_to_all x3, blocking collectives, exchange(): lax.all_to_all(array, axis, split_axis=0, concat_axis=0, axis_index_group...  61.2 us
    pallas_call x1, Pallas kernels, convolve(): on_device(conv_kernel, shape, cost, scratch)  2.77 us
    pallas_call x1, Pallas kernels, mix(): return on_device(kernel, shape, cost, scratch, in_specs=specs)(*held)  1.46 us

profile of v6, /device:TPU:1, one launch (start us, length us, event | category | flops | bytes accessed | tf_op | source)
XLA Modules:
  0.0 66.5 jit_solution(3668280078293587806)
XLA Ops:
  0.0 0.0 copy-start.2
  0.0 1.5 %shard_map.82 = bf16[32,32,256]{2,1,0:T(8,128)(2,1)S(1)} custom-call(bf16[256,512]{1,0:T(8,128)(2,1)} %k_hbm.1, bf16[256,512]{1,0:T(8,128)(2,1)} %v_hbm.1, f32[256,512]{1,0:T(8,128)} %filters_hbm.1), custom_call_target="tpu_custom_call" | custom-call | flops 131072 | bytes 1572864 | tf_op jit(solution)/shard_map/pallas_call | solution.py:278
  1.5 0.0 copy-start.3
  1.5 0.0 copy-start.4
  1.5 28.1 %all_to_all.15.in_ref = bf16[32,32,256]{2,1,0:T(8,128)(2,1)S(1)} all-to-all(bf16[32,32,256]{2,1,0:T(8,128)(2,1)S(1)} %shard_map.82), channel_id=1, replica_groups={{272,256,368,352,208,192,432,416,144,128,496,480,80,64,48,32,304,288,33..., dimensions={0} | all-to-all | bytes 1048576 | tf_op jit(solution)/shard_map/all_to_all | solution.py:322
  29.6 0.0 copy-done.2
  29.6 0.0 copy-done.3
  29.6 0.0 copy-done.4
  29.6 2.8 %shard_map.83 = bf16[32,16,256]{2,1,0:T(8,128)(2,1)S(1)} custom-call(bf16[32,32,256]{2,1,0:T(8,128)(2,1)S(1)} %all_to_all.15.in_ref, f32[2,33,256]{2,1,0:T(8,128)S(1)} %copy-done.4, bf16[3,512,256]{2,1,0:T(8,128)(2,1)S(1)} %copy-done.3, bf16[1024,512]{1,0:T(8,128)(2,1)S(1)} %copy-done.2), custom_call_target="tpu_custom_call" | custom-call | flops 1245708288 | bytes 2097152 | tf_op jit(solution)/shard_map/pallas_call | solution.py:298
  32.4 0.0 copy-start
  32.4 16.0 %all_to_all.16.conv_ref = bf16[32,16,256]{2,1,0:T(8,128)(2,1)S(1)} all-to-all(bf16[32,16,256]{2,1,0:T(8,128)(2,1)S(1)} %shard_map.83), channel_id=1, replica_groups={{272,368,208,432,144,496,80,48,304,336,240,400,176,464,112,16,256,352,1..., dimensions={0} | all-to-all | bytes 524288 | tf_op jit(solution)/shard_map/all_to_all | solution.py:322
  48.4 0.0 copy-done
  48.4 0.1 shard_map.84
  48.5 0.0 copy-start.1
  48.6 17.1 %all_to_all.17.rows_ref = bf16[16,16,512]{2,1,0:T(8,128)(2,1)S(1)} all-to-all(bf16[16,16,512]{2,1,0:T(8,128)(2,1)S(1)} %shard_map.84), channel_id=1, replica_groups={{9,11,7,13,5,15,3,1,8,10,6,12,4,14,2,0},{25,27,23,29,21,31,19,17,24,26,..., dimensions={0} | all-to-all | bytes 524288 | tf_op jit(solution)/shard_map/all_to_all | solution.py:322
  65.6 0.0 copy-done.1
  65.6 0.9 %shard_map.85 = bf16[16,8192]{1,0:T(8,128)(2,1)} custom-call(bf16[16,16,512]{2,1,0:T(8,128)(2,1)S(1)} %all_to_all.17.rows_ref, f32[1,8192]{1,0:T(1,128)S(1)} %bitcast.1), custom_call_target="tpu_custom_call" | custom-call | flops 786432 | bytes 557056 | tf_op jit(solution)/shard_map/pallas_call | solution.py:318
Async XLA Ops:
  0.0 29.6 %copy-start.2 = (bf16[1024,512]{1,0:T(8,128)(2,1)S(1)}, bf16[1024,512]{1,0:T(8,128)(2,1)}, u32[]{:S(2)}) copy-start(bf16[1024,512]{1,0:T(8,128)(2,1)} %constant.8.clone.outer_ref) | copy-start | bytes 3145732
  1.5 28.2 %copy-start.3 = (bf16[3,512,256]{2,1,0:T(8,128)(2,1)S(1)}, bf16[3,512,256]{2,1,0:T(8,128)(2,1)}, u32[]{:S(2)}) copy-start(bf16[3,512,256]{2,1,0:T(8,128)(2,1)} %constant.7.clone.inner_ref) | copy-start | bytes 2359300
  1.5 28.2 %copy-start.4 = (f32[2,33,256]{2,1,0:T(8,128)S(1)}, f32[2,33,256]{2,1,0:T(8,128)}, u32[]{:S(2)}) copy-start(f32[2,33,256]{2,1,0:T(8,128)} %constant.6.clone.twist_ref) | copy-start | bytes 202756
  32.4 16.0 %copy-start = (bf16[256,512]{1,0:T(8,128)(2,1)S(1)}, bf16[256,512]{1,0:T(8,128)(2,1)}, u32[]{:S(2)}) copy-start(bf16[256,512]{1,0:T(8,128)(2,1)} %q_ref.1) | copy-start | bytes 786436
  48.5 17.1 %copy-start.1 = (f32[8192]{0:T(1024)S(1)}, f32[8192]{0:T(1024)}, u32[]{:S(2)}) copy-start(f32[8192]{0:T(1024)} %param.12) | copy-start | bytes 98308

commit v7 on v5

--- a/solution.py
+++ b/solution.py
@@ -331,6 +331,14 @@
     return far
 
 
+def opposite(count):
+    return [n // 2 + n % 2 * (count // 2) for n in range(count)]
+
+
+def strided(count, step):
+    return [n * step % count for n in range(count)]
+
+
 def listed(places):
     return places[::-1]
 
@@ -341,7 +349,7 @@
         [
             z * 4 + (x + n) % 2 * 2 + core
             for x in range(2)
-            for n, z in enumerate(far_apart(ctx // 4))
+            for n, z in enumerate(opposite(ctx // 4))
             for core in range(2)
         ]
     )
@@ -350,7 +358,7 @@
             z * 4 + (x + n) % 2 * 2 + core
             for core in range(2)
             for x in range(2)
-            for n, z in enumerate(far_apart(ctx // 4))
+            for n, z in enumerate(strided(ctx // 4, 3))
         ]
     )
     order_ch = listed([y * 2 + x for x in range(2) for y in far_apart(ch // 2)])

time: 65.1 us -> 66 us (1.014)
  blocking collectives: 59.1 us -> 60.3 us
    all_to_all x3, blocking collectives: 59.1 us -> 60.3 us  [exchange(): lax.all_to_all(array, axis, split_axis=0, concat_axis=0, axis_index_group...]
where the time goes in v7:
time: 66 us; the launch traced here: 65.6 us
  blocking collectives  60.3 us (91%)
  Pallas kernels  5.22 us (8%)
    all_to_all x3, blocking collectives, exchange(): lax.all_to_all(array, axis, split_axis=0, concat_axis=0, axis_index_group...  60.3 us
    pallas_call x1, Pallas kernels, convolve(): on_device(conv_kernel, shape, cost, scratch)  2.77 us
    pallas_call x1, Pallas kernels, mix(): return on_device(kernel, shape, cost, scratch, in_specs=specs)(*held)  1.46 us

profile of v7, /device:TPU:6, one launch (start us, length us, event | category | flops | bytes accessed | tf_op | source)
XLA Modules:
  0.0 65.6 jit_solution(17169500688219541598)
XLA Ops:
  0.0 0.0 copy-start.2
  0.0 1.5 %shard_map.82 = bf16[32,32,256]{2,1,0:T(8,128)(2,1)S(1)} custom-call(bf16[256,512]{1,0:T(8,128)(2,1)} %k_hbm.1, bf16[256,512]{1,0:T(8,128)(2,1)} %v_hbm.1, f32[256,512]{1,0:T(8,128)} %filters_hbm.1), custom_call_target="tpu_custom_call" | custom-call | flops 131072 | bytes 1572864 | tf_op jit(solution)/shard_map/pallas_call | solution.py:278
  1.5 0.0 copy-start.3
  1.5 0.0 copy-start.4
  1.5 24.8 %all_to_all.15.in_ref = bf16[32,32,256]{2,1,0:T(8,128)(2,1)S(1)} all-to-all(bf16[32,32,256]{2,1,0:T(8,128)(2,1)S(1)} %shard_map.82), channel_id=1, replica_groups={{464,448,240,224,400,384,176,160,336,320,112,96,272,256,48,32,496,480,2..., dimensions={0} | all-to-all | bytes 1048576 | tf_op jit(solution)/shard_map/all_to_all | solution.py:322
  26.3 0.0 copy-done.2
  26.3 0.0 copy-done.3
  26.3 0.0 copy-done.4
  26.3 2.8 %shard_map.83 = bf16[32,16,256]{2,1,0:T(8,128)(2,1)S(1)} custom-call(bf16[32,32,256]{2,1,0:T(8,128)(2,1)S(1)} %all_to_all.15.in_ref, f32[2,33,256]{2,1,0:T(8,128)S(1)} %copy-done.4, bf16[3,512,256]{2,1,0:T(8,128)(2,1)S(1)} %copy-done.3, bf16[1024,512]{1,0:T(8,128)(2,1)S(1)} %copy-done.2), custom_call_target="tpu_custom_call" | custom-call | flops 1245708288 | bytes 2097152 | tf_op jit(solution)/shard_map/pallas_call | solution.py:298
  29.0 0.0 copy-start
  29.1 17.3 %all_to_all.16.conv_ref = bf16[32,16,256]{2,1,0:T(8,128)(2,1)S(1)} all-to-all(bf16[32,16,256]{2,1,0:T(8,128)(2,1)S(1)} %shard_map.83), channel_id=1, replica_groups={{336,176,464,304,80,432,208,48,368,144,496,272,112,400,240,16,320,160,4..., dimensions={0} | all-to-all | bytes 524288 | tf_op jit(solution)/shard_map/all_to_all | solution.py:322
  46.4 0.0 copy-done
  46.4 0.1 shard_map.84
  46.5 0.0 copy-start.1
  46.5 18.2 %all_to_all.17.rows_ref = bf16[16,16,512]{2,1,0:T(8,128)(2,1)S(1)} all-to-all(bf16[16,16,512]{2,1,0:T(8,128)(2,1)S(1)} %shard_map.84), channel_id=1, replica_groups={{15,7,11,3,13,5,9,1,14,6,10,2,12,4,8,0},{31,23,27,19,29,21,25,17,30,22,..., dimensions={0} | all-to-all | bytes 524288 | tf_op jit(solution)/shard_map/all_to_all | solution.py:322
  64.7 0.0 copy-done.1
  64.7 0.9 %shard_map.85 = bf16[16,8192]{1,0:T(8,128)(2,1)} custom-call(bf16[16,16,512]{2,1,0:T(8,128)(2,1)S(1)} %all_to_all.17.rows_ref, f32[1,8192]{1,0:T(1,128)S(1)} %bitcast.1), custom_call_target="tpu_custom_call" | custom-call | flops 786432 | bytes 557056 | tf_op jit(solution)/shard_map/pallas_call | solution.py:318
Async XLA Ops:
  0.0 26.3 %copy-start.2 = (bf16[1024,512]{1,0:T(8,128)(2,1)S(1)}, bf16[1024,512]{1,0:T(8,128)(2,1)}, u32[]{:S(2)}) copy-start(bf16[1024,512]{1,0:T(8,128)(2,1)} %constant.8.clone.outer_ref) | copy-start | bytes 3145732
  1.5 24.8 %copy-start.3 = (bf16[3,512,256]{2,1,0:T(8,128)(2,1)S(1)}, bf16[3,512,256]{2,1,0:T(8,128)(2,1)}, u32[]{:S(2)}) copy-start(bf16[3,512,256]{2,1,0:T(8,128)(2,1)} %constant.7.clone.inner_ref) | copy-start | bytes 2359300
  1.5 24.8 %copy-start.4 = (f32[2,33,256]{2,1,0:T(8,128)S(1)}, f32[2,33,256]{2,1,0:T(8,128)}, u32[]{:S(2)}) copy-start(f32[2,33,256]{2,1,0:T(8,128)} %constant.6.clone.twist_ref) | copy-start | bytes 202756
  29.0 17.3 %copy-start = (bf16[256,512]{1,0:T(8,128)(2,1)S(1)}, bf16[256,512]{1,0:T(8,128)(2,1)}, u32[]{:S(2)}) copy-start(bf16[256,512]{1,0:T(8,128)(2,1)} %q_ref.1) | copy-start | bytes 786436
  46.5 18.2 %copy-start.1 = (f32[8192]{0:T(1024)S(1)}, f32[8192]{0:T(1024)}, u32[]{:S(2)}) copy-start(f32[8192]{0:T(1024)} %param.12) | copy-start | bytes 98308

commit v8 on v7

--- a/solution.py
+++ b/solution.py
@@ -335,10 +335,6 @@
     return [n // 2 + n % 2 * (count // 2) for n in range(count)]
 
 
-def strided(count, step):
-    return [n * step % count for n in range(count)]
-
-
 def listed(places):
     return places[::-1]
 
@@ -358,7 +354,7 @@
             z * 4 + (x + n) % 2 * 2 + core
             for core in range(2)
             for x in range(2)
-            for n, z in enumerate(strided(ctx // 4, 3))
+            for n, z in enumerate(opposite(ctx // 4))
         ]
     )
     order_ch = listed([y * 2 + x for x in range(2) for y in far_apart(ch // 2)])

time: 66 us -> 65.2 us (0.988)
  blocking collectives: 60.3 us -> 59.4 us
    all_to_all x3, blocking collectives: 60.3 us -> 59.4 us  [exchange(): lax.all_to_all(array, axis, split_axis=0, concat_axis=0, axis_index_group...]
where the time goes in v8:
time: 65.2 us; the launch traced here: 64.7 us
  blocking collectives  59.4 us (91%)
  Pallas kernels  5.22 us (8%)
    all_to_all x3, blocking collectives, exchange(): lax.all_to_all(array, axis, split_axis=0, concat_axis=0, axis_index_group...  59.4 us
    pallas_call x1, Pallas kernels, convolve(): on_device(conv_kernel, shape, cost, scratch)  2.77 us
    pallas_call x1, Pallas kernels, mix(): return on_device(kernel, shape, cost, scratch, in_specs=specs)(*held)  1.46 us

profile of v8, /device:TPU:6, one launch (start us, length us, event | category | flops | bytes accessed | tf_op | source)
XLA Modules:
  0.0 64.7 jit_solution(7948909035107212400)
XLA Ops:
  0.0 0.0 copy-start.2
  0.0 1.5 %shard_map.82 = bf16[32,32,256]{2,1,0:T(8,128)(2,1)S(1)} custom-call(bf16[256,512]{1,0:T(8,128)(2,1)} %k_hbm.1, bf16[256,512]{1,0:T(8,128)(2,1)} %v_hbm.1, f32[256,512]{1,0:T(8,128)} %filters_hbm.1), custom_call_target="tpu_custom_call" | custom-call | flops 131072 | bytes 1572864 | tf_op jit(solution)/shard_map/pallas_call | solution.py:278
  1.5 0.0 copy-start.3
  1.5 0.0 copy-start.4
  1.5 24.8 %all_to_all.15.in_ref = bf16[32,32,256]{2,1,0:T(8,128)(2,1)S(1)} all-to-all(bf16[32,32,256]{2,1,0:T(8,128)(2,1)S(1)} %shard_map.82), channel_id=1, replica_groups={{464,448,240,224,400,384,176,160,336,320,112,96,272,256,48,32,496,480,2..., dimensions={0} | all-to-all | bytes 1048576 | tf_op jit(solution)/shard_map/all_to_all | solution.py:322
  26.3 0.0 copy-done.2
  26.3 0.0 copy-done.3
  26.3 0.0 copy-done.4
  26.3 2.8 %shard_map.83 = bf16[32,16,256]{2,1,0:T(8,128)(2,1)S(1)} custom-call(bf16[32,32,256]{2,1,0:T(8,128)(2,1)S(1)} %all_to_all.15.in_ref, f32[2,33,256]{2,1,0:T(8,128)S(1)} %copy-done.4, bf16[3,512,256]{2,1,0:T(8,128)(2,1)S(1)} %copy-done.3, bf16[1024,512]{1,0:T(8,128)(2,1)S(1)} %copy-done.2), custom_call_target="tpu_custom_call" | custom-call | flops 1245708288 | bytes 2097152 | tf_op jit(solution)/shard_map/pallas_call | solution.py:298
  29.0 0.0 copy-start
  29.1 15.5 %all_to_all.16.conv_ref = bf16[32,16,256]{2,1,0:T(8,128)(2,1)S(1)} all-to-all(bf16[32,16,256]{2,1,0:T(8,128)(2,1)S(1)} %shard_map.83), channel_id=1, replica_groups={{464,240,400,176,336,112,272,48,496,208,432,144,368,80,304,16,448,224,3..., dimensions={0} | all-to-all | bytes 524288 | tf_op jit(solution)/shard_map/all_to_all | solution.py:322
  44.6 0.0 copy-done
  44.6 0.1 shard_map.84
  44.7 0.0 copy-start.1
  44.7 19.2 %all_to_all.17.rows_ref = bf16[16,16,512]{2,1,0:T(8,128)(2,1)S(1)} all-to-all(bf16[16,16,512]{2,1,0:T(8,128)(2,1)S(1)} %shard_map.84), channel_id=1, replica_groups={{15,7,11,3,13,5,9,1,14,6,10,2,12,4,8,0},{31,23,27,19,29,21,25,17,30,22,..., dimensions={0} | all-to-all | bytes 524288 | tf_op jit(solution)/shard_map/all_to_all | solution.py:322
  63.9 0.0 copy-done.1
  63.9 0.9 %shard_map.85 = bf16[16,8192]{1,0:T(8,128)(2,1)} custom-call(bf16[16,16,512]{2,1,0:T(8,128)(2,1)S(1)} %all_to_all.17.rows_ref, f32[1,8192]{1,0:T(1,128)S(1)} %bitcast.1), custom_call_target="tpu_custom_call" | custom-call | flops 786432 | bytes 557056 | tf_op jit(solution)/shard_map/pallas_call | solution.py:318
Async XLA Ops:
  0.0 26.3 %copy-start.2 = (bf16[1024,512]{1,0:T(8,128)(2,1)S(1)}, bf16[1024,512]{1,0:T(8,128)(2,1)}, u32[]{:S(2)}) copy-start(bf16[1024,512]{1,0:T(8,128)(2,1)} %constant.8.clone.outer_ref) | copy-start | bytes 3145732
  1.5 24.8 %copy-start.3 = (bf16[3,512,256]{2,1,0:T(8,128)(2,1)S(1)}, bf16[3,512,256]{2,1,0:T(8,128)(2,1)}, u32[]{:S(2)}) copy-start(bf16[3,512,256]{2,1,0:T(8,128)(2,1)} %constant.7.clone.inner_ref) | copy-start | bytes 2359300
  1.5 24.8 %copy-start.4 = (f32[2,33,256]{2,1,0:T(8,128)S(1)}, f32[2,33,256]{2,1,0:T(8,128)}, u32[]{:S(2)}) copy-start(f32[2,33,256]{2,1,0:T(8,128)} %constant.6.clone.twist_ref) | copy-start | bytes 202756
  29.0 15.5 %copy-start = (bf16[256,512]{1,0:T(8,128)(2,1)S(1)}, bf16[256,512]{1,0:T(8,128)(2,1)}, u32[]{:S(2)}) copy-start(bf16[256,512]{1,0:T(8,128)(2,1)} %q_ref.1) | copy-start | bytes 786436
  44.7 19.2 %copy-start.1 = (f32[8192]{0:T(1024)S(1)}, f32[8192]{0:T(1024)}, u32[]{:S(2)}) copy-start(f32[8192]{0:T(1024)} %param.12) | copy-start | bytes 98308

commit v9 on v5

--- a/solution.py
+++ b/solution.py
@@ -331,6 +331,10 @@
     return far
 
 
+def opposite(count):
+    return [n // 2 + n % 2 * (count // 2) for n in range(count)]
+
+
 def listed(places):
     return places[::-1]
 
@@ -353,7 +357,7 @@
             for n, z in enumerate(far_apart(ctx // 4))
         ]
     )
-    order_ch = listed([y * 2 + x for x in range(2) for y in far_apart(ch // 2)])
+    order_ch = listed([y * 2 + x for x in range(2) for y in opposite(ch // 2)])
     pieces = exchange(mix(k_stream, v_stream, filters, order_in), "ctx", order_in)
     convolved = convolve(pieces, order_in, order_back)
     returned = exchange(convolved, "ctx", order_back)

time: 65.1 us -> 65.1 us (level)
  no operation moved by 1% of the time
where the time goes in v9:
time: 65.1 us; the launch traced here: 64.4 us
  blocking collectives  59.1 us (91%)
  Pallas kernels  5.22 us (8%)
    all_to_all x3, blocking collectives, exchange(): lax.all_to_all(array, axis, split_axis=0, concat_axis=0, axis_index_group...  59.1 us
    pallas_call x1, Pallas kernels, convolve(): on_device(conv_kernel, shape, cost, scratch)  2.77 us
    pallas_call x1, Pallas kernels, mix(): return on_device(kernel, shape, cost, scratch, in_specs=specs)(*held)  1.46 us

profile of v9, /device:TPU:6, one launch (start us, length us, event | category | flops | bytes accessed | tf_op | source)
XLA Modules:
  0.0 64.4 jit_solution(3675389545724085073)
XLA Ops:
  0.0 0.0 copy-start.2
  0.0 1.5 %shard_map.82 = bf16[32,32,256]{2,1,0:T(8,128)(2,1)S(1)} custom-call(bf16[256,512]{1,0:T(8,128)(2,1)} %k_hbm.1, bf16[256,512]{1,0:T(8,128)(2,1)} %v_hbm.1, f32[256,512]{1,0:T(8,128)} %filters_hbm.1), custom_call_target="tpu_custom_call" | custom-call | flops 131072 | bytes 1572864 | tf_op jit(solution)/shard_map/pallas_call | solution.py:278
  1.5 0.0 copy-start.3
  1.5 0.0 copy-start.4
  1.5 25.3 %all_to_all.15.in_ref = bf16[32,32,256]{2,1,0:T(8,128)(2,1)S(1)} all-to-all(bf16[32,32,256]{2,1,0:T(8,128)(2,1)S(1)} %shard_map.82), channel_id=1, replica_groups={{464,448,240,224,336,320,112,96,400,384,176,160,272,256,48,32,496,480,2..., dimensions={0} | all-to-all | bytes 1048576 | tf_op jit(solution)/shard_map/all_to_all | solution.py:322
  26.8 0.0 copy-done.2
  26.8 0.0 copy-done.3
  26.8 0.0 copy-done.4
  26.8 2.8 %shard_map.83 = bf16[32,16,256]{2,1,0:T(8,128)(2,1)S(1)} custom-call(bf16[32,32,256]{2,1,0:T(8,128)(2,1)S(1)} %all_to_all.15.in_ref, f32[2,33,256]{2,1,0:T(8,128)S(1)} %copy-done.4, bf16[3,512,256]{2,1,0:T(8,128)(2,1)S(1)} %copy-done.3, bf16[1024,512]{1,0:T(8,128)(2,1)S(1)} %copy-done.2), custom_call_target="tpu_custom_call" | custom-call | flops 1245708288 | bytes 2097152 | tf_op jit(solution)/shard_map/pallas_call | solution.py:298
  29.6 0.0 copy-start
  29.6 15.4 %all_to_all.16.conv_ref = bf16[32,16,256]{2,1,0:T(8,128)(2,1)S(1)} all-to-all(bf16[32,16,256]{2,1,0:T(8,128)(2,1)S(1)} %shard_map.83), channel_id=1, replica_groups={{464,240,336,112,400,176,272,48,496,208,368,80,432,144,304,16,448,224,3..., dimensions={0} | all-to-all | bytes 524288 | tf_op jit(solution)/shard_map/all_to_all | solution.py:322
  45.0 0.0 copy-done
  45.0 0.1 shard_map.84
  45.1 0.0 copy-start.1
  45.1 18.5 %all_to_all.17.rows_ref = bf16[16,16,512]{2,1,0:T(8,128)(2,1)S(1)} all-to-all(bf16[16,16,512]{2,1,0:T(8,128)(2,1)S(1)} %shard_map.84), channel_id=1, replica_groups={{15,7,13,5,11,3,9,1,14,6,12,4,10,2,8,0},{31,23,29,21,27,19,25,17,30,22,..., dimensions={0} | all-to-all | bytes 524288 | tf_op jit(solution)/shard_map/all_to_all | solution.py:322
  63.6 0.0 copy-done.1
  63.6 0.9 %shard_map.85 = bf16[16,8192]{1,0:T(8,128)(2,1)} custom-call(bf16[16,16,512]{2,1,0:T(8,128)(2,1)S(1)} %all_to_all.17.rows_ref, f32[1,8192]{1,0:T(1,128)S(1)} %bitcast.1), custom_call_target="tpu_custom_call" | custom-call | flops 786432 | bytes 557056 | tf_op jit(solution)/shard_map/pallas_call | solution.py:318
Async XLA Ops:
  0.0 26.8 %copy-start.2 = (bf16[1024,512]{1,0:T(8,128)(2,1)S(1)}, bf16[1024,512]{1,0:T(8,128)(2,1)}, u32[]{:S(2)}) copy-start(bf16[1024,512]{1,0:T(8,128)(2,1)} %constant.8.clone.outer_ref) | copy-start | bytes 3145732
  1.5 25.3 %copy-start.3 = (bf16[3,512,256]{2,1,0:T(8,128)(2,1)S(1)}, bf16[3,512,256]{2,1,0:T(8,128)(2,1)}, u32[]{:S(2)}) copy-start(bf16[3,512,256]{2,1,0:T(8,128)(2,1)} %constant.7.clone.inner_ref) | copy-start | bytes 2359300
  1.5 25.3 %copy-start.4 = (f32[2,33,256]{2,1,0:T(8,128)S(1)}, f32[2,33,256]{2,1,0:T(8,128)}, u32[]{:S(2)}) copy-start(f32[2,33,256]{2,1,0:T(8,128)} %constant.6.clone.twist_ref) | copy-start | bytes 202756
  29.6 15.4 %copy-start = (bf16[256,512]{1,0:T(8,128)(2,1)S(1)}, bf16[256,512]{1,0:T(8,128)(2,1)}, u32[]{:S(2)}) copy-start(bf16[256,512]{1,0:T(8,128)(2,1)} %q_ref.1) | copy-start | bytes 786436
  45.1 18.5 %copy-start.1 = (f32[8192]{0:T(1024)S(1)}, f32[8192]{0:T(1024)}, u32[]{:S(2)}) copy-start(f32[8192]{0:T(1024)} %param.12) | copy-start | bytes 98308

commit v10 on v9

--- a/solution.py
+++ b/solution.py
@@ -345,7 +345,7 @@
         [
             z * 4 + (x + n) % 2 * 2 + core
             for x in range(2)
-            for n, z in enumerate(far_apart(ctx // 4))
+            for n, z in enumerate(opposite(ctx // 4))
             for core in range(2)
         ]
     )

time: 65.1 us -> 65 us (level)
  no operation moved by 1% of the time
where the time goes in v10:
time: 65 us; the launch traced here: 64.4 us
  blocking collectives  59 us (91%)
  Pallas kernels  5.22 us (8%)
    all_to_all x3, blocking collectives, exchange(): lax.all_to_all(array, axis, split_axis=0, concat_axis=0, axis_index_group...  59 us
    pallas_call x1, Pallas kernels, convolve(): on_device(conv_kernel, shape, cost, scratch)  2.77 us
    pallas_call x1, Pallas kernels, mix(): return on_device(kernel, shape, cost, scratch, in_specs=specs)(*held)  1.46 us

profile of v10, /device:TPU:6, one launch (start us, length us, event | category | flops | bytes accessed | tf_op | source)
XLA Modules:
  0.0 64.4 jit_solution(8099674109443767099)
XLA Ops:
  0.0 0.0 copy-start.2
  0.0 1.5 %shard_map.82 = bf16[32,32,256]{2,1,0:T(8,128)(2,1)S(1)} custom-call(bf16[256,512]{1,0:T(8,128)(2,1)} %k_hbm.1, bf16[256,512]{1,0:T(8,128)(2,1)} %v_hbm.1, f32[256,512]{1,0:T(8,128)} %filters_hbm.1), custom_call_target="tpu_custom_call" | custom-call | flops 131072 | bytes 1572864 | tf_op jit(solution)/shard_map/pallas_call | solution.py:278
  1.5 0.0 copy-start.3
  1.5 0.0 copy-start.4
  1.5 24.8 %all_to_all.15.in_ref = bf16[32,32,256]{2,1,0:T(8,128)(2,1)S(1)} all-to-all(bf16[32,32,256]{2,1,0:T(8,128)(2,1)S(1)} %shard_map.82), channel_id=1, replica_groups={{464,448,240,224,400,384,176,160,336,320,112,96,272,256,48,32,496,480,2..., dimensions={0} | all-to-all | bytes 1048576 | tf_op jit(solution)/shard_map/all_to_all | solution.py:322
  26.3 0.0 copy-done.2
  26.3 0.0 copy-done.3
  26.3 0.0 copy-done.4
  26.3 2.8 %shard_map.83 = bf16[32,16,256]{2,1,0:T(8,128)(2,1)S(1)} custom-call(bf16[32,32,256]{2,1,0:T(8,128)(2,1)S(1)} %all_to_all.15.in_ref, f32[2,33,256]{2,1,0:T(8,128)S(1)} %copy-done.4, bf16[3,512,256]{2,1,0:T(8,128)(2,1)S(1)} %copy-done.3, bf16[1024,512]{1,0:T(8,128)(2,1)S(1)} %copy-done.2), custom_call_target="tpu_custom_call" | custom-call | flops 1245708288 | bytes 2097152 | tf_op jit(solution)/shard_map/pallas_call | solution.py:298
  29.0 0.0 copy-start
  29.1 15.8 %all_to_all.16.conv_ref = bf16[32,16,256]{2,1,0:T(8,128)(2,1)S(1)} all-to-all(bf16[32,16,256]{2,1,0:T(8,128)(2,1)S(1)} %shard_map.83), channel_id=1, replica_groups={{464,240,336,112,400,176,272,48,496,208,368,80,432,144,304,16,448,224,3..., dimensions={0} | all-to-all | bytes 524288 | tf_op jit(solution)/shard_map/all_to_all | solution.py:322
  44.8 0.0 copy-done
  44.8 0.1 shard_map.84
  45.0 0.0 copy-start.1
  45.0 18.5 %all_to_all.17.rows_ref = bf16[16,16,512]{2,1,0:T(8,128)(2,1)S(1)} all-to-all(bf16[16,16,512]{2,1,0:T(8,128)(2,1)S(1)} %shard_map.84), channel_id=1, replica_groups={{15,7,13,5,11,3,9,1,14,6,12,4,10,2,8,0},{31,23,29,21,27,19,25,17,30,22,..., dimensions={0} | all-to-all | bytes 524288 | tf_op jit(solution)/shard_map/all_to_all | solution.py:322
  63.5 0.0 copy-done.1
  63.5 0.9 %shard_map.85 = bf16[16,8192]{1,0:T(8,128)(2,1)} custom-call(bf16[16,16,512]{2,1,0:T(8,128)(2,1)S(1)} %all_to_all.17.rows_ref, f32[1,8192]{1,0:T(1,128)S(1)} %bitcast.1), custom_call_target="tpu_custom_call" | custom-call | flops 786432 | bytes 557056 | tf_op jit(solution)/shard_map/pallas_call | solution.py:318
Async XLA Ops:
  0.0 26.3 %copy-start.2 = (bf16[1024,512]{1,0:T(8,128)(2,1)S(1)}, bf16[1024,512]{1,0:T(8,128)(2,1)}, u32[]{:S(2)}) copy-start(bf16[1024,512]{1,0:T(8,128)(2,1)} %constant.8.clone.outer_ref) | copy-start | bytes 3145732
  1.5 24.8 %copy-start.3 = (bf16[3,512,256]{2,1,0:T(8,128)(2,1)S(1)}, bf16[3,512,256]{2,1,0:T(8,128)(2,1)}, u32[]{:S(2)}) copy-start(bf16[3,512,256]{2,1,0:T(8,128)(2,1)} %constant.7.clone.inner_ref) | copy-start | bytes 2359300
  1.5 24.8 %copy-start.4 = (f32[2,33,256]{2,1,0:T(8,128)S(1)}, f32[2,33,256]{2,1,0:T(8,128)}, u32[]{:S(2)}) copy-start(f32[2,33,256]{2,1,0:T(8,128)} %constant.6.clone.twist_ref) | copy-start | bytes 202756
  29.0 15.8 %copy-start = (bf16[256,512]{1,0:T(8,128)(2,1)S(1)}, bf16[256,512]{1,0:T(8,128)(2,1)}, u32[]{:S(2)}) copy-start(bf16[256,512]{1,0:T(8,128)(2,1)} %q_ref.1) | copy-start | bytes 786436
  45.0 18.5 %copy-start.1 = (f32[8192]{0:T(1024)S(1)}, f32[8192]{0:T(1024)}, u32[]{:S(2)}) copy-start(f32[8192]{0:T(1024)} %param.12) | copy-start | bytes 98308

commit v11 on v9

--- a/solution.py
+++ b/solution.py
@@ -357,7 +357,9 @@
             for n, z in enumerate(far_apart(ctx // 4))
         ]
     )
-    order_ch = listed([y * 2 + x for x in range(2) for y in opposite(ch // 2)])
+    planes = opposite(ch // 2)
+    rounds = (planes[: ch // 4], planes[ch // 4 :])
+    order_ch = listed([y * 2 + x for part in rounds for x in range(2) for y in part])
     pieces = exchange(mix(k_stream, v_stream, filters, order_in), "ctx", order_in)
     convolved = convolve(pieces, order_in, order_back)
     returned = exchange(convolved, "ctx", order_back)

time: 65.1 us -> 65.1 us (level)
  no operation moved by 1% of the time
where the time goes in v11:
time: 65.1 us; the launch traced here: 64.3 us
  blocking collectives  59 us (91%)
  Pallas kernels  5.22 us (8%)
    all_to_all x3, blocking collectives, exchange(): lax.all_to_all(array, axis, split_axis=0, concat_axis=0, axis_index_group...  59 us
    pallas_call x1, Pallas kernels, convolve(): on_device(conv_kernel, shape, cost, scratch)  2.77 us
    pallas_call x1, Pallas kernels, mix(): return on_device(kernel, shape, cost, scratch, in_specs=specs)(*held)  1.46 us

profile of v11, /device:TPU:6, one launch (start us, length us, event | category | flops | bytes accessed | tf_op | source)
XLA Modules:
  0.0 64.3 jit_solution(13141938379869337996)
XLA Ops:
  0.0 0.0 copy-start.2
  0.0 1.5 %shard_map.82 = bf16[32,32,256]{2,1,0:T(8,128)(2,1)S(1)} custom-call(bf16[256,512]{1,0:T(8,128)(2,1)} %k_hbm.1, bf16[256,512]{1,0:T(8,128)(2,1)} %v_hbm.1, f32[256,512]{1,0:T(8,128)} %filters_hbm.1), custom_call_target="tpu_custom_call" | custom-call | flops 131072 | bytes 1572864 | tf_op jit(solution)/shard_map/pallas_call | solution.py:278
  1.5 0.0 copy-start.3
  1.5 0.0 copy-start.4
  1.5 25.3 %all_to_all.15.in_ref = bf16[32,32,256]{2,1,0:T(8,128)(2,1)S(1)} all-to-all(bf16[32,32,256]{2,1,0:T(8,128)(2,1)S(1)} %shard_map.82), channel_id=1, replica_groups={{464,448,240,224,336,320,112,96,400,384,176,160,272,256,48,32,496,480,2..., dimensions={0} | all-to-all | bytes 1048576 | tf_op jit(solution)/shard_map/all_to_all | solution.py:322
  26.8 0.0 copy-done.2
  26.8 0.0 copy-done.3
  26.8 0.0 copy-done.4
  26.8 2.8 %shard_map.83 = bf16[32,16,256]{2,1,0:T(8,128)(2,1)S(1)} custom-call(bf16[32,32,256]{2,1,0:T(8,128)(2,1)S(1)} %all_to_all.15.in_ref, f32[2,33,256]{2,1,0:T(8,128)S(1)} %copy-done.4, bf16[3,512,256]{2,1,0:T(8,128)(2,1)S(1)} %copy-done.3, bf16[1024,512]{1,0:T(8,128)(2,1)S(1)} %copy-done.2), custom_call_target="tpu_custom_call" | custom-call | flops 1245708288 | bytes 2097152 | tf_op jit(solution)/shard_map/pallas_call | solution.py:298
  29.6 0.0 copy-start
  29.6 15.4 %all_to_all.16.conv_ref = bf16[32,16,256]{2,1,0:T(8,128)(2,1)S(1)} all-to-all(bf16[32,16,256]{2,1,0:T(8,128)(2,1)S(1)} %shard_map.83), channel_id=1, replica_groups={{464,240,336,112,400,176,272,48,496,208,368,80,432,144,304,16,448,224,3..., dimensions={0} | all-to-all | bytes 524288 | tf_op jit(solution)/shard_map/all_to_all | solution.py:322
  45.0 0.0 copy-done
  45.0 0.1 shard_map.84
  45.1 0.0 copy-start.1
  45.1 18.3 %all_to_all.17.rows_ref = bf16[16,16,512]{2,1,0:T(8,128)(2,1)S(1)} all-to-all(bf16[16,16,512]{2,1,0:T(8,128)(2,1)S(1)} %shard_map.84), channel_id=1, replica_groups={{15,7,13,5,14,6,12,4,11,3,9,1,10,2,8,0},{31,23,29,21,30,22,28,20,27,19,..., dimensions={0} | all-to-all | bytes 524288 | tf_op jit(solution)/shard_map/all_to_all | solution.py:322
  63.4 0.0 copy-done.1
  63.4 0.9 %shard_map.85 = bf16[16,8192]{1,0:T(8,128)(2,1)} custom-call(bf16[16,16,512]{2,1,0:T(8,128)(2,1)S(1)} %all_to_all.17.rows_ref, f32[1,8192]{1,0:T(1,128)S(1)} %bitcast.1), custom_call_target="tpu_custom_call" | custom-call | flops 786432 | bytes 557056 | tf_op jit(solution)/shard_map/pallas_call | solution.py:318
Async XLA Ops:
  0.0 26.8 %copy-start.2 = (bf16[1024,512]{1,0:T(8,128)(2,1)S(1)}, bf16[1024,512]{1,0:T(8,128)(2,1)}, u32[]{:S(2)}) copy-start(bf16[1024,512]{1,0:T(8,128)(2,1)} %constant.8.clone.outer_ref) | copy-start | bytes 3145732
  1.5 25.3 %copy-start.3 = (bf16[3,512,256]{2,1,0:T(8,128)(2,1)S(1)}, bf16[3,512,256]{2,1,0:T(8,128)(2,1)}, u32[]{:S(2)}) copy-start(bf16[3,512,256]{2,1,0:T(8,128)(2,1)} %constant.7.clone.inner_ref) | copy-start | bytes 2359300
  1.5 25.3 %copy-start.4 = (f32[2,33,256]{2,1,0:T(8,128)S(1)}, f32[2,33,256]{2,1,0:T(8,128)}, u32[]{:S(2)}) copy-start(f32[2,33,256]{2,1,0:T(8,128)} %constant.6.clone.twist_ref) | copy-start | bytes 202756
  29.6 15.4 %copy-start = (bf16[256,512]{1,0:T(8,128)(2,1)S(1)}, bf16[256,512]{1,0:T(8,128)(2,1)}, u32[]{:S(2)}) copy-start(bf16[256,512]{1,0:T(8,128)(2,1)} %q_ref.1) | copy-start | bytes 786436
  45.1 18.3 %copy-start.1 = (f32[8192]{0:T(1024)S(1)}, f32[8192]{0:T(1024)}, u32[]{:S(2)}) copy-start(f32[8192]{0:T(1024)} %param.12) | copy-start | bytes 98308
